TPU v7x, 512 devices: a whole 4x4x16 slice. The times are simulated.
512 devices in a mesh: leaf: 64 (over y, z), front: 8 (over x, core).
Axes of the slice: x: 4, y: 4, z: 16, core: 2. Of those that a mesh axis runs over, the one named last changes fastest.
Arguments:
- leaf_rhs: bfloat16 [64, 256, 4, 512], P('leaf', 'front'), may hold values from -6 to 6
- sep_rhs: bfloat16 [64, 512, 768], P('leaf', 'front'), may hold values from -6 to 6
- leaf_noise: bfloat16 [64, 256, 4, 512], P('leaf', 'front'), may hold values from -6 to 6
- sep_noise: bfloat16 [64, 512, 768], P('leaf', 'front'), may hold values from -6 to 6
- leaf_inverse: bfloat16 [64, 4, 256, 256], P('leaf', None, 'front'), as said below
- leaf_left: bfloat16 [64, 4, 256, 768], P('leaf', None, 'front'), may hold values from -0.09375 to 0.09375
- leaf_right: bfloat16 [64, 4, 256, 768], P('leaf', None, 'front'), may hold values from -0.09375 to 0.09375
- sep_inverse: bfloat16 [64, 768, 768], P('leaf'), as said below
- sep_left: bfloat16 [64, 768, 768], P('leaf'), may hold values from -0.109375 to 0.109375
- sep_right: bfloat16 [64, 768, 768], P('leaf'), may hold values from -0.109375 to 0.109375
- leaf_count: int32 [64], P('leaf'), may hold values from 1 to 4, as said below
Outputs:
- leaf_draws: float32 [64, 256, 4, 512], P('leaf', 'front')
- sep_draws: float32 [64, 512, 768], P('leaf', 'front')
Inputs may be any that keep to these rules, and one draw needn't show every extreme that they name: `leaf_count`: every section has at least one live leaf supernode, and some section has 4. `leaf_inverse`: each block is lower triangular with a positive diagonal. `sep_inverse`: each block is lower triangular with a positive diagonal.
All inputs are finite; a program needn't handle non-finite values.
Results may differ from a plain program's by a relative error of at most 0.034.
Values may be sent and summed in bfloat16 or wider, within the bound.
A program may use at most 64 MiB of HBM per device.

v0:
```python
import jax
import jax.numpy as jnp
from jax import lax
from jax.sharding import PartitionSpec as P


def shifted(value, axis, steps):
    count = lax.axis_size(axis)
    first, last = (max(0, -steps), min(count, count - steps))
    return lax.ppermute(value, axis, [(source, source + steps) for source in range(first, last)])


def send_upward(values, distance):
    return shifted(values.astype(jnp.bfloat16), "leaf", distance).astype(values.dtype)


def send_downward(values, distance):
    return shifted(values, "leaf", distance)


def on_device(
    leaf_rhs,
    sep_rhs,
    leaf_noise,
    sep_noise,
    leaf_inverse,
    leaf_left,
    leaf_right,
    sep_inverse,
    sep_left,
    sep_right,
    leaf_count,
):
    depth_levels = lax.axis_size("leaf").bit_length() - 1
    position = lax.axis_index("leaf") + 1
    tree_level = jnp.zeros((), jnp.int32)
    for bit_index in range(1, depth_levels + 1):
        tree_level = tree_level + (position % 2**bit_index == 0).astype(jnp.int32)
    live_slots = leaf_count[0]
    inverse_rows = leaf_inverse[0]
    left_cols = leaf_left[0]
    right_cols = leaf_right[0]
    sep_inv = sep_inverse[0]
    up_left = sep_left[0]
    up_right = sep_right[0]
    slot_active = jnp.arange(inverse_rows.shape[0]) < live_slots
    own_rhs = leaf_rhs[0]
    own_sep = sep_rhs[0]
    own_noise = leaf_noise[0]
    own_sep_noise = sep_noise[0]
    row_share, slots, samples = own_rhs.shape
    share = own_sep.shape[0]
    width = own_sep.shape[1]
    start_sums = jnp.zeros((row_share, slots, samples), jnp.float32)
    shard_piece = lax.all_gather(own_rhs, "front", axis=0, tiled=True)

    def one_slot(slot, totals):
        slot_rows = lax.dynamic_index_in_dim(inverse_rows, slot, 0, keepdims=False)
        column = lax.dynamic_index_in_dim(shard_piece, slot, 1, keepdims=False)
        previous = lax.dynamic_index_in_dim(totals, slot, 1, keepdims=False)
        product = jnp.dot(slot_rows, column, preferred_element_type=jnp.float32)
        return lax.dynamic_update_index_in_dim(totals, previous + product, slot, 1)

    solved_leaf = lax.fori_loop(0, live_slots, one_slot, start_sums).astype(jnp.bfloat16)
    sample_part = solved_leaf
    toward_right = jnp.einsum(
        "stc,tsp->cp", sample_part, right_cols, preferred_element_type=jnp.float32
    )
    toward_left = jnp.einsum(
        "stc,tsp->cp", sample_part, left_cols, preferred_element_type=jnp.float32
    )
    summed = lax.psum_scatter(
        jnp.concatenate([toward_right, toward_left], axis=1).astype(jnp.bfloat16),
        "front",
        scatter_dimension=0,
        tiled=True,
    ).astype(jnp.float32)
    from_next = shifted(summed[:, width:].astype(jnp.bfloat16), "leaf", -1).astype(jnp.float32)
    residual = own_sep.astype(jnp.float32) - summed[:, :width] - from_next
    solved_sep = jnp.zeros((share, width), jnp.bfloat16)
    for height in range(depth_levels + 1):
        at_level = tree_level == height
        candidate = lax.dot_general(
            residual.astype(jnp.bfloat16),
            sep_inv,
            (((1,), (1,)), ((), ())),
            preferred_element_type=jnp.float32,
        ).astype(jnp.bfloat16)
        solved_sep = jnp.where(at_level, candidate, solved_sep)
        if height < depth_levels:
            send_right = jnp.where(
                at_level, jnp.dot(solved_sep, up_right, preferred_element_type=jnp.float32), 0.0
            )
            send_left = jnp.where(
                at_level, jnp.dot(solved_sep, up_left, preferred_element_type=jnp.float32), 0.0
            )
            got_right = send_upward(send_right, 2**height)
            got_left = send_upward(send_left, -(2**height))
            residual = residual - got_right - got_left
    solved_leaf, solved_sep = (solved_leaf, solved_sep)
    target = solved_sep.astype(jnp.float32) + own_sep_noise.astype(jnp.float32)
    draws_sep = jnp.zeros(target.shape, jnp.float32)
    rounded_sep = jnp.zeros(target.shape, jnp.bfloat16)
    for height in range(depth_levels, -1, -1):
        at_level = tree_level == height
        if height < depth_levels:
            from_below = send_downward(rounded_sep, 2**height)
            from_above = send_downward(rounded_sep, -(2**height))
            pulled_sep = lax.dot_general(
                from_below, up_left, (((1,), (1,)), ((), ())), preferred_element_type=jnp.float32
            )
            pulled_sep = pulled_sep + lax.dot_general(
                from_above, up_right, (((1,), (1,)), ((), ())), preferred_element_type=jnp.float32
            )
            combined = target - pulled_sep
        else:
            combined = target
        candidate = jnp.dot(
            combined.astype(jnp.bfloat16), sep_inv, preferred_element_type=jnp.float32
        )
        draws_sep = jnp.where(at_level, candidate, draws_sep)
        rounded_sep = draws_sep.astype(jnp.bfloat16)
    previous_sep = shifted(rounded_sep, "leaf", 1)
    stacked = jnp.stack([rounded_sep, previous_sep])
    pull_shard_piece = lax.all_gather(stacked, "front", axis=1, tiled=True)
    own_side = jnp.einsum(
        "tsp,cp->stc", right_cols, pull_shard_piece[0], preferred_element_type=jnp.float32
    )
    other_side = jnp.einsum(
        "tsp,cp->stc", left_cols, pull_shard_piece[1], preferred_element_type=jnp.float32
    )
    pulled_leaf = own_side + other_side
    mixed = jnp.where(
        slot_active[None, :, None],
        solved_leaf.astype(jnp.float32) + own_noise.astype(jnp.float32) - pulled_leaf,
        0.0,
    ).astype(jnp.bfloat16)
    draws_leaf = lax.psum_scatter(
        jnp.einsum("tgs,gtc->stc", inverse_rows, mixed, preferred_element_type=jnp.float32).astype(
            jnp.bfloat16
        ),
        "front",
        scatter_dimension=0,
        tiled=True,
    ).astype(jnp.float32)
    draws_leaf, draws_sep = (draws_leaf, draws_sep)
    return (draws_leaf[None], draws_sep[None])


def solution(mesh):
    return jax.shard_map(
        on_device,
        mesh=mesh,
        in_specs=(
            P("leaf", "front", None, None),
            P("leaf", "front", None),
            P("leaf", "front", None, None),
            P("leaf", "front", None),
            P("leaf", None, "front", None),
            P("leaf", None, "front", None),
            P("leaf", None, "front", None),
            P("leaf", None, None),
            P("leaf", None, None),
            P("leaf", None, None),
            P("leaf"),
        ),
        out_specs=(P("leaf", "front", None, None), P("leaf", "front", None)),
        check_vma=False,
    )
```

profile of v0, /device:TPU:1, one launch (start us, length us, event | category | flops | bytes accessed | tf_op | source)
XLA Modules:
  0.0 451.6 jit_solution(13301859249138541515)
XLA Ops:
  7.2 1.7 copy.18
  9.0 38.7 %all-gather.6.cloned.1.call-done = bf16[1,256,4,512]{3,1,2,0:T(8,128)(2,1)} async-done(((bf16[1,32,4,512]{3,1,2,0:T(8,128)(2,1)}), bf16[1,256,4,512]{3,1,2,0:T(8,128)(2,1)}) %all-gather.6.cloned.1.call-update) | async-done | bytes 1048592 | tf_op jit(solution)/shard_map/all_gather | solution.py:55
  47.7 4.3 while.10
  53.5 1.3 pad_maximum_fusion
  54.9 40.2 %reduce-scatter.2.cloned.1.call-done = bf16[64,1536]{1,0:T(8,128)(2,1)} async-done(((bf16[512,1536]{1,0:T(8,128)(2,1)}), bf16[64,1536]{1,0:T(8,128)(2,1)}) %reduce-scatter.2.cloned.1.call-update) | async-done | bytes 196624 | tf_op jit(solution)/shard_map/reduce_scatter | solution.py:72
  95.0 1.5 slice.22
  97.9 4.3 collective-permute-done
  102.2 1.5 fusion.292
  107.0 4.6 %collective-permute-start.1 = (bf16[64,768]{1,0:T(8,128)(2,1)}, bf16[64,768]{1,0:T(8,128)(2,1)}, u32[]{:S(2)}, u32[]{:S(2)}) collective-permute-start(bf16[64,768]{1,0:T(8,128)(2,1)} %fusion.253), channel_id=1, source_target_pairs={{0,8},{8,16},{16,24},{24,32},{32,40},{40,48},{48,56},{56,64},{64,7... | collective-permute-start | bytes 294920 | tf_op jit(solution)/shard_map/ppermute | solution.py:10
  114.1 1.5 fusion.289
  118.8 5.5 %collective-permute-start.3 = (bf16[64,768]{1,0:T(8,128)(2,1)}, bf16[64,768]{1,0:T(8,128)(2,1)}, u32[]{:S(2)}, u32[]{:S(2)}) collective-permute-start(bf16[64,768]{1,0:T(8,128)(2,1)} %fusion.250), channel_id=1, source_target_pairs={{0,16},{8,24},{16,32},{24,40},{32,48},{40,56},{48,64},{56,72},{64,... | collective-permute-start | bytes 294920 | tf_op jit(solution)/shard_map/ppermute | solution.py:10
  124.4 1.3 collective-permute-done.3
  125.7 1.6 fusion.286
  130.5 12.4 %collective-permute-start.5 = (bf16[64,768]{1,0:T(8,128)(2,1)}, bf16[64,768]{1,0:T(8,128)(2,1)}, u32[]{:S(2)}, u32[]{:S(2)}) collective-permute-start(bf16[64,768]{1,0:T(8,128)(2,1)} %fusion.247), channel_id=1, source_target_pairs={{0,32},{8,40},{16,48},{24,56},{32,64},{40,72},{48,80},{56,88},{64,... | collective-permute-start | bytes 294920 | tf_op jit(solution)/shard_map/ppermute | solution.py:10
  142.9 1.3 collective-permute-done.5
  145.4 1.5 fusion.283
  150.1 16.7 %collective-permute-start.7 = (bf16[64,768]{1,0:T(8,128)(2,1)}, bf16[64,768]{1,0:T(8,128)(2,1)}, u32[]{:S(2)}, u32[]{:S(2)}) collective-permute-start(bf16[64,768]{1,0:T(8,128)(2,1)} %fusion.244), channel_id=1, source_target_pairs={{0,64},{8,72},{16,80},{24,88},{32,96},{40,104},{48,112},{56,120},{... | collective-permute-start | bytes 294920 | tf_op jit(solution)/shard_map/ppermute | solution.py:10
  166.9 3.2 collective-permute-done.7
  170.1 1.6 fusion.280
  174.9 15.1 %collective-permute-start.9 = (bf16[64,768]{1,0:T(8,128)(2,1)}, bf16[64,768]{1,0:T(8,128)(2,1)}, u32[]{:S(2)}, u32[]{:S(2)}) collective-permute-start(bf16[64,768]{1,0:T(8,128)(2,1)} %fusion.241), channel_id=1, source_target_pairs={{0,128},{8,136},{16,144},{24,152},{32,160},{40,168},{48,176},{56,1... | collective-permute-start | bytes 294920 | tf_op jit(solution)/shard_map/ppermute | solution.py:10
  191.3 1.7 fusion.277
  196.3 7.1 %collective-permute-start.11 = (bf16[64,768]{1,0:T(8,128)(2,1)}, bf16[64,768]{1,0:T(8,128)(2,1)}, u32[]{:S(2)}, u32[]{:S(2)}) collective-permute-start(bf16[64,768]{1,0:T(8,128)(2,1)} %fusion.238), channel_id=1, source_target_pairs={{0,256},{8,264},{16,272},{24,280},{32,288},{40,296},{48,304},{56,3... | collective-permute-start | bytes 294920 | tf_op jit(solution)/shard_map/ppermute | solution.py:10
  203.4 1.3 collective-permute-done.11
  204.7 1.8 fusion.274
  208.8 5.5 %collective-permute-start.13 = (bf16[64,768]{1,0:T(8,128)(2,1)S(1)}, bf16[64,768]{1,0:T(8,128)(2,1)S(1)}, u32[]{:S(2)}, u32[]{:S(2)}) collective-permute-start(bf16[64,768]{1,0:T(8,128)(2,1)S(1)} %get-tuple-element.45), channel_id=1, source_target_pairs={{0,256},{8,264},{16,272},{24,280},{32,288},{40,296},{48,304},{56,3... | collective-permute-start | bytes 294920 | tf_op jit(solution)/shard_map/ppermute | solution.py:10
  216.9 2.6 fusion.323
  220.8 4.6 %collective-permute-start.15 = (bf16[64,768]{1,0:T(8,128)(2,1)}, bf16[64,768]{1,0:T(8,128)(2,1)}, u32[]{:S(2)}, u32[]{:S(2)}) collective-permute-start(bf16[64,768]{1,0:T(8,128)(2,1)} %get-tuple-element.47), channel_id=1, source_target_pairs={{0,128},{8,136},{16,144},{24,152},{32,160},{40,168},{48,176},{56,1... | collective-permute-start | bytes 294920 | tf_op jit(solution)/shard_map/ppermute | solution.py:10
  226.7 2.6 fusion.326
  230.6 13.3 %collective-permute-start.17 = (bf16[64,768]{1,0:T(8,128)(2,1)}, bf16[64,768]{1,0:T(8,128)(2,1)}, u32[]{:S(2)}, u32[]{:S(2)}) collective-permute-start(bf16[64,768]{1,0:T(8,128)(2,1)} %get-tuple-element.49), channel_id=1, source_target_pairs={{0,64},{8,72},{16,80},{24,88},{32,96},{40,104},{48,112},{56,120},{... | collective-permute-start | bytes 294920 | tf_op jit(solution)/shard_map/ppermute | solution.py:10
  245.2 3.2 collective-permute-done.17
  248.4 2.6 fusion.329
  252.3 9.3 %collective-permute-start.19 = (bf16[64,768]{1,0:T(8,128)(2,1)}, bf16[64,768]{1,0:T(8,128)(2,1)}, u32[]{:S(2)}, u32[]{:S(2)}) collective-permute-start(bf16[64,768]{1,0:T(8,128)(2,1)} %get-tuple-element.51), channel_id=1, source_target_pairs={{0,32},{8,40},{16,48},{24,56},{32,64},{40,72},{48,80},{56,88},{64,... | collective-permute-start | bytes 294920 | tf_op jit(solution)/shard_map/ppermute | solution.py:10
  263.7 2.9 collective-permute-done.19
  266.6 2.6 fusion.332
  270.5 10.9 %collective-permute-start.21 = (bf16[64,768]{1,0:T(8,128)(2,1)}, bf16[64,768]{1,0:T(8,128)(2,1)}, u32[]{:S(2)}, u32[]{:S(2)}) collective-permute-start(bf16[64,768]{1,0:T(8,128)(2,1)} %get-tuple-element.53), channel_id=1, source_target_pairs={{0,16},{8,24},{16,32},{24,40},{32,48},{40,56},{48,64},{56,72},{64,... | collective-permute-start | bytes 294920 | tf_op jit(solution)/shard_map/ppermute | solution.py:10
  281.4 1.4 collective-permute-done.22
  283.9 2.6 fusion.335
  287.9 4.0 collective-permute-start.23
  291.9 1.3 collective-permute-done.24
  296.2 2.5 fusion.338
  298.7 3.9 collective-permute-start.25
  302.7 1.6 collective-permute-done.25
  305.7 56.0 %all-gather.4.cloned.1.call-done = bf16[2,512,768]{2,1,0:T(8,128)(2,1)} async-done(((bf16[2,64,768]{2,1,0:T(8,128)(2,1)}), bf16[2,512,768]{2,1,0:T(8,128)(2,1)}) %all-gather.4.cloned.1.call-update) | async-done | bytes 1572880 | tf_op jit(solution)/shard_map/all_gather | solution.py:125
  361.7 1.5 fusion.295
  363.2 2.0 fusion.7
  365.3 1.8 copy.20
  369.0 74.4 %all-reduce.3.cloned.1.call-done = bf16[256,4,512]{2,1,0:T(4,128)(2,1)} async-done(((bf16[256,4,512]{2,1,0:T(4,128)(2,1)}), bf16[256,4,512]{2,1,0:T(4,128)(2,1)}) %all-reduce.3.cloned.1.call-update) | async-done | bytes 1048592
  443.4 1.6 bitcast_convert_fusion.2
  (112 shorter events, 51.6 us)
Async XLA Ops:
  7.2 95.1 %copy-start = (bf16[1,768,768]{2,1,0:T(8,128)(2,1)S(1)}, bf16[1,768,768]{2,1,0:T(8,128)(2,1)}, u32[]{:S(2)}) copy-start(bf16[1,768,768]{2,1,0:T(8,128)(2,1)} %param.20) | copy-start | bytes 3538948
  7.2 40.5 %all-gather.6.cloned.1.call-start = ((), (), s32[]{:S(2)}) async-start(), calls=%async_computation.3 | async-start | bytes 1179648 | tf_op jit(solution)/shard_map/all_gather | solution.py:55
  8.9 86.1 %reduce-scatter.2.cloned.1.call-start = ((), (), s32[]{:S(2)}) async-start(), calls=%async_computation.1 | async-start | bytes 1769472 | tf_op jit(solution)/shard_map/reduce_scatter | solution.py:72
  47.7 4.4 copy-start.15
  54.8 48.9 %copy-start.2 = (bf16[1,768,768]{2,1,0:T(8,128)(2,1)S(1)}, bf16[1,768,768]{2,1,0:T(8,128)(2,1)}, u32[]{:S(2)}) copy-start(bf16[1,768,768]{2,1,0:T(8,128)(2,1)} %param.21) | copy-start | bytes 3538948
  54.8 306.8 %all-gather.4.cloned.1.call-start = ((), (), s32[]{:S(2)}) async-start(), calls=%async_computation.2 | async-start | bytes 1769472 | tf_op jit(solution)/shard_map/all_gather | solution.py:125
  96.6 5.7 %collective-permute-start = (bf16[64,768]{1,0:T(8,128)(2,1)}, bf16[64,768]{1,0:T(8,128)(2,1)}, u32[]{:S(2)}, u32[]{:S(2)}) collective-permute-start(bf16[64,768]{1,0:T(8,128)(2,1)} %slice.22), channel_id=1, source_target_pairs={{8,0},{16,8},{24,16},{32,24},{40,32},{48,40},{56,48},{64,56},{72,6... | collective-permute-start | bytes 294920 | tf_op jit(solution)/shard_map/ppermute | solution.py:10
  97.9 8.1 %copy-start.1 = (bf16[1,768,768]{2,1,0:T(8,128)(2,1)S(1)}, bf16[1,768,768]{2,1,0:T(8,128)(2,1)}, u32[]{:S(2)}) copy-start(bf16[1,768,768]{2,1,0:T(8,128)(2,1)} %param.22) | copy-start | bytes 3538948
  103.7 3.3 copy-start.9
  104.7 6.9 %collective-permute-start.2 = (bf16[64,768]{1,0:T(8,128)(2,1)}, bf16[64,768]{1,0:T(8,128)(2,1)}, u32[]{:S(2)}, u32[]{:S(2)}) collective-permute-start(bf16[64,768]{1,0:T(8,128)(2,1)} %fusion.235), channel_id=1, source_target_pairs={{8,0},{16,8},{24,16},{32,24},{40,32},{48,40},{56,48},{64,56},{72,6... | collective-permute-start | bytes 294920 | tf_op jit(solution)/shard_map/ppermute | solution.py:10
  107.0 5.9 %collective-permute-start.1 = (bf16[64,768]{1,0:T(8,128)(2,1)}, bf16[64,768]{1,0:T(8,128)(2,1)}, u32[]{:S(2)}, u32[]{:S(2)}) collective-permute-start(bf16[64,768]{1,0:T(8,128)(2,1)} %fusion.253), channel_id=1, source_target_pairs={{0,8},{8,16},{16,24},{24,32},{32,40},{40,48},{48,56},{56,64},{64,7... | collective-permute-start | bytes 294920 | tf_op jit(solution)/shard_map/ppermute | solution.py:10
  114.1 2.5 copy-start.5
  115.6 2.0 copy-start.12
  117.5 6.8 %collective-permute-start.4 = (bf16[64,768]{1,0:T(8,128)(2,1)}, bf16[64,768]{1,0:T(8,128)(2,1)}, u32[]{:S(2)}, u32[]{:S(2)}) collective-permute-start(bf16[64,768]{1,0:T(8,128)(2,1)} %fusion.232), channel_id=1, source_target_pairs={{16,0},{24,8},{32,16},{40,24},{48,32},{56,40},{64,48},{72,56},{80,... | collective-permute-start | bytes 294920 | tf_op jit(solution)/shard_map/ppermute | solution.py:10
  118.8 6.8 %collective-permute-start.3 = (bf16[64,768]{1,0:T(8,128)(2,1)}, bf16[64,768]{1,0:T(8,128)(2,1)}, u32[]{:S(2)}, u32[]{:S(2)}) collective-permute-start(bf16[64,768]{1,0:T(8,128)(2,1)} %fusion.250), channel_id=1, source_target_pairs={{0,16},{8,24},{16,32},{24,40},{32,48},{40,56},{48,64},{56,72},{64,... | collective-permute-start | bytes 294920 | tf_op jit(solution)/shard_map/ppermute | solution.py:10
  127.3 2.0 copy-start.11
  129.2 13.6 %collective-permute-start.6 = (bf16[64,768]{1,0:T(8,128)(2,1)}, bf16[64,768]{1,0:T(8,128)(2,1)}, u32[]{:S(2)}, u32[]{:S(2)}) collective-permute-start(bf16[64,768]{1,0:T(8,128)(2,1)} %fusion.229), channel_id=1, source_target_pairs={{32,0},{40,8},{48,16},{56,24},{64,32},{72,40},{80,48},{88,56},{96,... | collective-permute-start | bytes 294920 | tf_op jit(solution)/shard_map/ppermute | solution.py:10
  130.5 13.7 %collective-permute-start.5 = (bf16[64,768]{1,0:T(8,128)(2,1)}, bf16[64,768]{1,0:T(8,128)(2,1)}, u32[]{:S(2)}, u32[]{:S(2)}) collective-permute-start(bf16[64,768]{1,0:T(8,128)(2,1)} %fusion.247), channel_id=1, source_target_pairs={{0,32},{8,40},{16,48},{24,56},{32,64},{40,72},{48,80},{56,88},{64,... | collective-permute-start | bytes 294920 | tf_op jit(solution)/shard_map/ppermute | solution.py:10
  145.4 2.5 copy-start.4
  146.8 2.0 copy-start.13
  148.8 18.1 %collective-permute-start.8 = (bf16[64,768]{1,0:T(8,128)(2,1)}, bf16[64,768]{1,0:T(8,128)(2,1)}, u32[]{:S(2)}, u32[]{:S(2)}) collective-permute-start(bf16[64,768]{1,0:T(8,128)(2,1)} %fusion.226), channel_id=1, source_target_pairs={{64,0},{72,8},{80,16},{88,24},{96,32},{104,40},{112,48},{120,56},{... | collective-permute-start | bytes 294920 | tf_op jit(solution)/shard_map/ppermute | solution.py:10
  150.1 20.0 %collective-permute-start.7 = (bf16[64,768]{1,0:T(8,128)(2,1)}, bf16[64,768]{1,0:T(8,128)(2,1)}, u32[]{:S(2)}, u32[]{:S(2)}) collective-permute-start(bf16[64,768]{1,0:T(8,128)(2,1)} %fusion.244), channel_id=1, source_target_pairs={{0,64},{8,72},{16,80},{24,88},{32,96},{40,104},{48,112},{56,120},{... | collective-permute-start | bytes 294920 | tf_op jit(solution)/shard_map/ppermute | solution.py:10
  171.7 2.0 copy-start.10
  173.6 16.4 %collective-permute-start.10 = (bf16[64,768]{1,0:T(8,128)(2,1)}, bf16[64,768]{1,0:T(8,128)(2,1)}, u32[]{:S(2)}, u32[]{:S(2)}) collective-permute-start(bf16[64,768]{1,0:T(8,128)(2,1)} %fusion.223), channel_id=1, source_target_pairs={{128,0},{136,8},{144,16},{152,24},{160,32},{168,40},{176,48},{184,... | collective-permute-start | bytes 294920 | tf_op jit(solution)/shard_map/ppermute | solution.py:10
  174.9 16.4 %collective-permute-start.9 = (bf16[64,768]{1,0:T(8,128)(2,1)}, bf16[64,768]{1,0:T(8,128)(2,1)}, u32[]{:S(2)}, u32[]{:S(2)}) collective-permute-start(bf16[64,768]{1,0:T(8,128)(2,1)} %fusion.241), channel_id=1, source_target_pairs={{0,128},{8,136},{16,144},{24,152},{32,160},{40,168},{48,176},{56,1... | collective-permute-start | bytes 294920 | tf_op jit(solution)/shard_map/ppermute | solution.py:10
  193.0 2.0 copy-start.8
  195.0 8.4 %collective-permute-start.12 = (bf16[64,768]{1,0:T(8,128)(2,1)}, bf16[64,768]{1,0:T(8,128)(2,1)}, u32[]{:S(2)}, u32[]{:S(2)}) collective-permute-start(bf16[64,768]{1,0:T(8,128)(2,1)} %fusion.220), channel_id=1, source_target_pairs={{256,0},{264,8},{272,16},{280,24},{288,32},{296,40},{304,48},{312,... | collective-permute-start | bytes 294920 | tf_op jit(solution)/shard_map/ppermute | solution.py:10
  196.3 8.4 %collective-permute-start.11 = (bf16[64,768]{1,0:T(8,128)(2,1)}, bf16[64,768]{1,0:T(8,128)(2,1)}, u32[]{:S(2)}, u32[]{:S(2)}) collective-permute-start(bf16[64,768]{1,0:T(8,128)(2,1)} %fusion.238), channel_id=1, source_target_pairs={{0,256},{8,264},{16,272},{24,280},{32,288},{40,296},{48,304},{56,3... | collective-permute-start | bytes 294920 | tf_op jit(solution)/shard_map/ppermute | solution.py:10
  206.5 9.8 %copy-start.3 = (f32[64,768]{1,0:T(8,128)}, f32[64,768]{1,0:T(8,128)S(1)}, u32[]{:S(2)}) copy-start(f32[64,768]{1,0:T(8,128)S(1)} %fusion.274) | copy-start | bytes 589828
  207.5 7.6 %collective-permute-start.14 = (bf16[64,768]{1,0:T(8,128)(2,1)S(1)}, bf16[64,768]{1,0:T(8,128)(2,1)S(1)}, u32[]{:S(2)}, u32[]{:S(2)}) collective-permute-start(bf16[64,768]{1,0:T(8,128)(2,1)S(1)} %get-tuple-element.45), channel_id=1, source_target_pairs={{256,0},{264,8},{272,16},{280,24},{288,32},{296,40},{304,48},{312,... | collective-permute-start | bytes 294920 | tf_op jit(solution)/shard_map/ppermute | solution.py:10
  208.8 7.5 %collective-permute-start.13 = (bf16[64,768]{1,0:T(8,128)(2,1)S(1)}, bf16[64,768]{1,0:T(8,128)(2,1)S(1)}, u32[]{:S(2)}, u32[]{:S(2)}) collective-permute-start(bf16[64,768]{1,0:T(8,128)(2,1)S(1)} %get-tuple-element.45), channel_id=1, source_target_pairs={{0,256},{8,264},{16,272},{24,280},{32,288},{40,296},{48,304},{56,3... | collective-permute-start | bytes 294920 | tf_op jit(solution)/shard_map/ppermute | solution.py:10
  219.5 5.9 %collective-permute-start.16 = (bf16[64,768]{1,0:T(8,128)(2,1)}, bf16[64,768]{1,0:T(8,128)(2,1)S(1)}, u32[]{:S(2)}, u32[]{:S(2)}) collective-permute-start(bf16[64,768]{1,0:T(8,128)(2,1)} %get-tuple-element.47), channel_id=1, source_target_pairs={{128,0},{136,8},{144,16},{152,24},{160,32},{168,40},{176,48},{184,... | collective-permute-start | bytes 294920 | tf_op jit(solution)/shard_map/ppermute | solution.py:10
  220.8 5.9 %collective-permute-start.15 = (bf16[64,768]{1,0:T(8,128)(2,1)}, bf16[64,768]{1,0:T(8,128)(2,1)}, u32[]{:S(2)}, u32[]{:S(2)}) collective-permute-start(bf16[64,768]{1,0:T(8,128)(2,1)} %get-tuple-element.47), channel_id=1, source_target_pairs={{0,128},{8,136},{16,144},{24,152},{32,160},{40,168},{48,176},{56,1... | collective-permute-start | bytes 294920 | tf_op jit(solution)/shard_map/ppermute | solution.py:10
  229.4 14.6 %collective-permute-start.18 = (bf16[64,768]{1,0:T(8,128)(2,1)}, bf16[64,768]{1,0:T(8,128)(2,1)S(1)}, u32[]{:S(2)}, u32[]{:S(2)}) collective-permute-start(bf16[64,768]{1,0:T(8,128)(2,1)} %get-tuple-element.49), channel_id=1, source_target_pairs={{64,0},{72,8},{80,16},{88,24},{96,32},{104,40},{112,48},{120,56},{... | collective-permute-start | bytes 294920 | tf_op jit(solution)/shard_map/ppermute | solution.py:10
  230.6 17.8 %collective-permute-start.17 = (bf16[64,768]{1,0:T(8,128)(2,1)}, bf16[64,768]{1,0:T(8,128)(2,1)}, u32[]{:S(2)}, u32[]{:S(2)}) collective-permute-start(bf16[64,768]{1,0:T(8,128)(2,1)} %get-tuple-element.49), channel_id=1, source_target_pairs={{0,64},{8,72},{16,80},{24,88},{32,96},{40,104},{48,112},{56,120},{... | collective-permute-start | bytes 294920 | tf_op jit(solution)/shard_map/ppermute | solution.py:10
  251.0 11.4 %collective-permute-start.20 = (bf16[64,768]{1,0:T(8,128)(2,1)}, bf16[64,768]{1,0:T(8,128)(2,1)S(1)}, u32[]{:S(2)}, u32[]{:S(2)}) collective-permute-start(bf16[64,768]{1,0:T(8,128)(2,1)} %get-tuple-element.51), channel_id=1, source_target_pairs={{32,0},{40,8},{48,16},{56,24},{64,32},{72,40},{80,48},{88,56},{96,... | collective-permute-start | bytes 294920 | tf_op jit(solution)/shard_map/ppermute | solution.py:10
  252.3 14.2 %collective-permute-start.19 = (bf16[64,768]{1,0:T(8,128)(2,1)}, bf16[64,768]{1,0:T(8,128)(2,1)}, u32[]{:S(2)}, u32[]{:S(2)}) collective-permute-start(bf16[64,768]{1,0:T(8,128)(2,1)} %get-tuple-element.51), channel_id=1, source_target_pairs={{0,32},{8,40},{16,48},{24,56},{32,64},{40,72},{48,80},{56,88},{64,... | collective-permute-start | bytes 294920 | tf_op jit(solution)/shard_map/ppermute | solution.py:10
  269.2 13.6 %collective-permute-start.22 = (bf16[64,768]{1,0:T(8,128)(2,1)}, bf16[64,768]{1,0:T(8,128)(2,1)S(1)}, u32[]{:S(2)}, u32[]{:S(2)}) collective-permute-start(bf16[64,768]{1,0:T(8,128)(2,1)} %get-tuple-element.53), channel_id=1, source_target_pairs={{16,0},{24,8},{32,16},{40,24},{48,32},{56,40},{64,48},{72,56},{80,... | collective-permute-start | bytes 294920 | tf_op jit(solution)/shard_map/ppermute | solution.py:10
  270.5 13.5 %collective-permute-start.21 = (bf16[64,768]{1,0:T(8,128)(2,1)}, bf16[64,768]{1,0:T(8,128)(2,1)}, u32[]{:S(2)}, u32[]{:S(2)}) collective-permute-start(bf16[64,768]{1,0:T(8,128)(2,1)} %get-tuple-element.53), channel_id=1, source_target_pairs={{0,16},{8,24},{16,32},{24,40},{32,48},{40,56},{48,64},{56,72},{64,... | collective-permute-start | bytes 294920 | tf_op jit(solution)/shard_map/ppermute | solution.py:10
  286.6 6.6 %collective-permute-start.24 = (bf16[64,768]{1,0:T(8,128)(2,1)}, bf16[64,768]{1,0:T(8,128)(2,1)S(1)}, u32[]{:S(2)}, u32[]{:S(2)}) collective-permute-start(bf16[64,768]{1,0:T(8,128)(2,1)} %get-tuple-element.55), channel_id=1, source_target_pairs={{8,0},{16,8},{24,16},{32,24},{40,32},{48,40},{56,48},{64,56},{72,6... | collective-permute-start | bytes 294920 | tf_op jit(solution)/shard_map/ppermute | solution.py:10
  287.9 7.7 %collective-permute-start.23 = (bf16[64,768]{1,0:T(8,128)(2,1)}, bf16[64,768]{1,0:T(8,128)(2,1)S(1)}, u32[]{:S(2)}, u32[]{:S(2)}) collective-permute-start(bf16[64,768]{1,0:T(8,128)(2,1)} %get-tuple-element.55), channel_id=1, source_target_pairs={{0,8},{8,16},{16,24},{24,32},{32,40},{40,48},{48,56},{56,64},{64,7... | collective-permute-start | bytes 294920 | tf_op jit(solution)/shard_map/ppermute | solution.py:10
  296.2 65.5 %copy-start.21 = (bf16[1,4,32,768]{3,2,1,0:T(8,128)(2,1)S(1)}, bf16[1,4,32,768]{3,2,1,0:T(8,128)(2,1)}, u32[]{:S(2)}) copy-start(bf16[1,4,32,768]{3,2,1,0:T(8,128)(2,1)} %param.19) | copy-start | bytes 589828
  298.7 64.5 %copy-start.7 = (f32[32,4,512]{2,0,1:T(8,128)S(1)}, f32[32,4,512]{2,0,1:T(8,128)}, u32[]{:S(2)}) copy-start(f32[32,4,512]{2,0,1:T(8,128)} %copy-done.6) | copy-start | bytes 786436
  298.7 64.5 %copy-start.14 = (bf16[4,32,256]{2,1,0:T(8,128)(2,1)S(1)}, bf16[4,32,256]{2,1,0:T(8,128)(2,1)}, u32[]{:S(2)}) copy-start(bf16[4,32,256]{2,1,0:T(8,128)(2,1)} %get-tuple-element.131) | copy-start | bytes 196612
  298.7 64.5 %copy-start.16 = (bf16[1,4,32,768]{3,2,1,0:T(8,128)(2,1)S(1)}, bf16[1,4,32,768]{3,2,1,0:T(8,128)(2,1)}, u32[]{:S(2)}) copy-start(bf16[1,4,32,768]{3,2,1,0:T(8,128)(2,1)} %param.18) | copy-start | bytes 589828
  298.7 64.5 %copy-start.17 = (bf16[1,32,4,512]{3,2,1,0:T(4,128)(2,1)S(1)}, bf16[1,32,4,512]{3,2,1,0:T(4,128)(2,1)}, u32[]{:S(2)}) copy-start(bf16[1,32,4,512]{3,2,1,0:T(4,128)(2,1)} %param.15) | copy-start | bytes 393220
  298.7 5.6 %collective-permute-start.25 = (bf16[64,768]{1,0:T(8,128)(2,1)S(1)}, bf16[64,768]{1,0:T(8,128)(2,1)S(1)}, u32[]{:S(2)}, u32[]{:S(2)}) collective-permute-start(bf16[64,768]{1,0:T(8,128)(2,1)S(1)} %get-tuple-element.57), channel_id=1, source_target_pairs={{0,8},{8,16},{16,24},{24,32},{32,40},{40,48},{48,56},{56,64},{64,7... | collective-permute-start | bytes 294920 | tf_op jit(solution)/shard_map/ppermute | solution.py:10
  305.0 138.5 %all-reduce.3.cloned.1.call-start = ((), (), s32[]{:S(2)}) async-start(), calls=%async_computation.4 | async-start | bytes 2097152
  (4 other events, 3.7 us)
Sparse Core Ops, SparseCore 0:
  10.7 36.9 all-gather.5
  54.9 40.0 reduce-scatter.1
  305.1 56.4 all-gather.3
  367.2 76.1 all-reduce.2
where the time goes:
time: 455 us; the launch traced here: 452 us
  waiting for transfers between devices  237 us (52%)
  starting transfers between devices  130 us (29%)
  matrix products  53.1 us (12%)
  between operations  15.6 us (3%)
  local copies, waits for them, and re-layouts  8.32 us (2%)
  other arithmetic  5.95 us (1%)
    ppermute x26, starting transfers between devices, shifted(): lax.ppermute(value, axis, [(source, source + steps) for source in range(f...  130 us
    unnamed x5, waiting for transfers between devices  74.5 us
    all_gather x1, waiting for transfers between devices, on_device(): pull_shard_piece = lax.all_gather(stacked, 'front', axis=1, tiled=True)  56 us
    reduce_scatter x1, waiting for transfers between devices, on_device(): lax.psum_scatter(jnp.concatenate([toward_right, toward_left], axis=1).ast...  40.2 us
    all_gather x1, waiting for transfers between devices, on_device(): shard_piece = lax.all_gather(own_rhs, 'front', axis=0, tiled=True)  38.7 us
    ppermute x26, waiting for transfers between devices, shifted(): lax.ppermute(value, axis, [(source, source + steps) for source in range(f...  27.4 us
    dot_general x7, matrix products, on_device(): jnp.dot(combined.astype(jnp.bfloat16), sep_inv, preferred_element_type=jn...  16.6 us
    dot_general x7, matrix products, on_device(): lax.dot_general(residual.astype(jnp.bfloat16), sep_inv, (((1,), (1,)), ((...  11 us
  transfers between devices with their start and end apart: 30, of which 21 were waited for; matrix products, arithmetic and copies ran while one was open for 2% of the time, Pallas kernels for 0%

commit v1 on v0

v1 whole, which is shorter than its diff:
```python
import functools

import jax
import jax.numpy as jnp
from jax import lax
from jax.experimental import pallas as pl
from jax.experimental.pallas import tpu as pltpu
from jax.sharding import PartitionSpec as P

MESH = pl.DeviceIdType.MESH
BF = jnp.bfloat16
F32 = jnp.float32
HALF = 64


def nn(a, b):
    return lax.dot_general(a, b, (((1,), (0,)), ((), ())), preferred_element_type=F32)


def nt(a, b):
    return lax.dot_general(a, b, (((1,), (1,)), ((), ())), preferred_element_type=F32)


def tn(a, b):
    return lax.dot_general(a, b, (((0,), (0,)), ((), ())), preferred_element_type=F32)


def pack(block_ref, packed_ref):
    _, rows, samples = block_ref.shape
    for slab in range(samples // 128):
        lanes = slice(slab * 128, slab * 128 + 128)
        a = block_ref[0:2, :, lanes].reshape(2 * rows, 128)
        b = block_ref[2:4, :, lanes].reshape(2 * rows, 128)
        for core in range(2):
            part = slice(core * HALF, core * HALF + HALF)
            both = jnp.concatenate([a[:, part], b[:, part]], axis=1)
            packed_ref[2 * slab + core] = both.reshape(2, rows, 128)


def kernel(
    n_leaf,
    n_front,
    depth,
    cnt_ref,
    rhs_hbm,
    noise_hbm,
    inv_hbm,
    left_hbm,
    right_hbm,
    srhs_hbm,
    snoise_hbm,
    sinv_hbm,
    sleft_hbm,
    sright_hbm,
    leaf_out,
    sep_out,
    x_buf,
    n_buf,
    pk,
    pkn,
    r2,
    n2,
    inv,
    lw,
    srhs,
    snoise,
    sinv,
    su,
    w,
    s2,
    res,
    rb,
    zacc,
    tl_send,
    tl_recv,
    up_send,
    up_recv,
    dn_send,
    dn_recv,
    own_dup,
    prev_dup,
    pull,
    d2,
    o2,
    load_sem,
    a_send,
    a_recv,
    nz_send,
    nz_recv,
    gi_send,
    gi_recv,
    g_send,
    g_recv,
    tl_ssem,
    tl_rsem,
    up_ssem,
    up_rsem,
    dn_ssem,
    dn_rsem,
    o_send,
    o_recv,
):
    leaf = lax.axis_index("leaf")
    front = lax.axis_index("front")
    chips = n_front // 2
    x = front // 2
    core = front % 2
    rows = x_buf.shape[1]
    pos = leaf + 1
    level = jnp.int32(0)
    for bit in range(1, depth + 1):
        level = level + (pos % (1 << bit) == 0).astype(jnp.int32)
    span = jnp.int32(1)
    for bit in range(1, depth + 1):
        span = jnp.where(pos % (1 << bit) == 0, jnp.int32(1 << bit), span)
    odd = leaf % 2
    is_even = odd == 0

    def inside(target):
        return jnp.logical_and(target >= 0, target < n_leaf)

    def load(i, src, dst):
        return pltpu.make_async_copy(src, dst, load_sem.at[i])

    own_rows = pl.ds(pl.multiple_of(front * rows, rows), rows)
    loads = [
        load(0, rhs_hbm, x_buf),
        load(1, inv_hbm, inv.at[:, own_rows, :]),
        load(2, right_hbm, lw.at[0, :, own_rows, :]),
        load(3, left_hbm, lw.at[1, :, own_rows, :]),
        load(4, sinv_hbm, sinv),
        load(5, sleft_hbm, su.at[0]),
        load(6, sright_hbm, su.at[1]),
        load(7, srhs_hbm, srhs),
        load(8, snoise_hbm, snoise),
        load(9, noise_hbm, n_buf),
    ]
    for copy in loads:
        copy.start()

    barrier = pltpu.get_barrier_semaphore()
    partners = jnp.int32(n_front - 1)
    for step in range(1, n_front):
        pl.semaphore_signal(
            barrier, inc=1, device_id={"front": (front + step) % n_front}, device_id_type=MESH
        )
    for h in range(depth + 1):
        for sign in (-1, 1):
            target = leaf + sign * (1 << h)
            reached = jnp.logical_and(h <= level, inside(target))
            partners = partners + reached.astype(jnp.int32)

            @pl.when(reached)
            def _():
                pl.semaphore_signal(
                    barrier, inc=1, device_id={"leaf": target}, device_id_type=MESH
                )

    pl.semaphore_wait(barrier, partners)

    def exchange(src, dst_at, sends, recvs, step):
        peer = (front + step) % n_front
        return pltpu.make_async_remote_copy(
            src_ref=src.at[peer],
            dst_ref=dst_at(front),
            send_sem=sends.at[step - 1],
            recv_sem=recvs.at[step - 1],
            device_id={"front": peer},
            device_id_type=MESH,
        )

    def arrival(src, dst_at, sends, recvs, step):
        peer = (front + n_front - step) % n_front
        return pltpu.make_async_remote_copy(
            src_ref=src.at[peer],
            dst_ref=dst_at(peer),
            send_sem=sends.at[step - 1],
            recv_sem=recvs.at[step - 1],
            device_id={"front": peer},
            device_id_type=MESH,
        )

    def rows_of(ref):
        return lambda f: ref.at[:, pl.ds(pl.multiple_of(f * rows, rows), rows), :]

    def piece(buf, dx, flip, low, high):
        chip = (x + dx + chips) % chips
        who = 2 * chip + (1 - core if flip else core)
        return buf.at[low:high, pl.ds(pl.multiple_of(who * rows, rows), rows), :]

    routes = [
        (0, 0, 4, 1, False),
        (0, 0, 4, -1, False),
        (0, 0, 4, 0, True),
        (-1, 0, 4, 0, True),
        (-1, 0, 2, 1, False),
        (1, 0, 4, 0, True),
        (1, 2, 4, -1, False),
        (2, 0, 2, 0, True),
        (2, 2, 4, 0, True),
    ]

    def route(buf, sends, recvs, i):
        dx, low, high, to, flip = routes[i]
        chip = (x + to + chips) % chips
        peer = 2 * chip + (1 - core if flip else core)
        block = piece(buf, dx, False, low, high)
        return pltpu.make_async_remote_copy(
            src_ref=block,
            dst_ref=block,
            send_sem=sends.at[i],
            recv_sem=recvs.at[i],
            device_id={"front": peer},
            device_id_type=MESH,
        )

    def route_arrival(buf, sends, recvs, i):
        dx, low, high, to, flip = routes[i]
        chip = (x + to + chips) % chips
        peer = 2 * chip + (1 - core if flip else core)
        block = piece(buf, dx - to, flip, low, high)
        return pltpu.make_async_remote_copy(
            src_ref=block,
            dst_ref=block,
            send_sem=sends.at[i],
            recv_sem=recvs.at[i],
            device_id={"front": peer},
            device_id_type=MESH,
        )

    class Gather:
        def __init__(self, buf, sends, recvs):
            self.args = (buf, sends, recvs)

        def send(self, *which):
            for i in which:
                route(*self.args, i).start()

        def take(self, *which):
            for i in which:
                route_arrival(*self.args, i).wait_recv()

        def drain(self):
            for i in range(len(routes)):
                route(*self.args, i).wait_send()

    first = odd
    second = 1 - odd
    gather_inv = Gather(inv, gi_send, gi_recv)
    gather_one = Gather(lw.at[first], g_send.at[0], g_recv.at[0])
    gather_two = Gather(lw.at[second], g_send.at[1], g_recv.at[1])

    loads[0].wait()
    pack(x_buf, pk)
    for step in range(1, n_front):
        exchange(pk, rows_of(r2), a_send, a_recv, step).start()
    loads[1].wait()
    gather_inv.send(0, 1, 2)
    loads[2].wait()
    loads[3].wait()
    gather_one.send(0, 1, 2)
    r2[:, own_rows, :] = pk[front]

    loads[4].wait()
    loads[5].wait()
    w[0] = tn(sinv[...], su[0]).astype(BF)
    gather_inv.take(0)
    gather_inv.send(4, 3)
    gather_inv.take(1)
    gather_inv.send(6, 5)
    loads[6].wait()
    w[1] = tn(sinv[...], su[1]).astype(BF)
    gather_one.take(0)
    gather_one.send(4, 3)
    gather_one.take(1)
    gather_one.send(6, 5)
    gather_inv.take(4)
    gather_inv.send(7)
    gather_inv.take(6)
    gather_inv.send(8)
    gather_two.send(0, 1, 2)
    for step in range(1, n_front):
        arrival(pk, rows_of(r2), a_send, a_recv, step).wait_recv()
    gather_inv.take(2, 3, 5, 7, 8)

    live = cnt_ref[0]
    low_lanes = lax.broadcasted_iota(jnp.int32, (1, 128), 1) < HALF
    alive = [
        jnp.logical_or(
            jnp.logical_and(low_lanes, t < live),
            jnp.logical_and(jnp.logical_not(low_lanes), t + 2 < live),
        )
        for t in range(2)
    ]
    for t in range(2):
        block = r2[t]
        solved = jnp.where(low_lanes, nn(inv[t], block), nn(inv[t + 2], block))
        s2[t] = jnp.where(alive[t], solved, 0.0).astype(BF)

    def toward(side):
        total = jnp.zeros((HALF, srhs.shape[1]), F32)
        for t in range(2):
            turned = s2[t].T
            total = total + nn(turned[0:HALF], lw[side, t])
            total = total + nn(turned[HALF:], lw[side, t + 2])
        return total

    def tl_copy(target):
        return pltpu.make_async_remote_copy(
            src_ref=tl_send,
            dst_ref=tl_recv,
            send_sem=tl_ssem,
            recv_sem=tl_rsem,
            device_id={"leaf": target},
            device_id_type=MESH,
        )

    def up_copy(i, h, target):
        return pltpu.make_async_remote_copy(
            src_ref=up_send.at[i],
            dst_ref=up_recv.at[h, i],
            send_sem=up_ssem.at[i],
            recv_sem=up_rsem.at[h, i],
            device_id={"leaf": target},
            device_id_type=MESH,
        )

    def dn_copy(i, h, target):
        return pltpu.make_async_remote_copy(
            src_ref=dn_send,
            dst_ref=dn_recv.at[i],
            send_sem=dn_ssem.at[i, h],
            recv_sem=dn_rsem.at[i],
            device_id={"leaf": target},
            device_id_type=MESH,
        )

    near = ((pos // span) % 4 == 1).astype(jnp.int32)
    own_level = jnp.minimum(level, depth - 1)

    def ancestor(i):
        return leaf + (2 * i - 1) * span

    def climb():
        rb[...] = res[...].astype(BF)
        for j in range(2):
            i = near if j == 0 else 1 - near
            target = ancestor(i)

            @pl.when(inside(target))
            def _():
                up_send[i] = nn(rb[...], w[i]).astype(BF)
                up_copy(i, own_level, target).start()

    gather_one.take(4)
    gather_one.send(7)
    gather_one.take(6)
    gather_one.send(8)
    gather_one.take(2, 3, 5, 7, 8)
    loads[7].wait()
    part_one = toward(first)

    @pl.when(is_even)
    def _():
        res[...] = srhs[...].astype(F32) - part_one
        tl_copy(leaf + 1).wait_recv()
        res[...] = res[...] - tl_recv[...].astype(F32)
        climb()

    @pl.when(jnp.logical_not(is_even))
    def _():
        tl_send[...] = part_one.astype(BF)
        tl_copy(leaf - 1).start()

    gather_two.take(0)
    gather_two.send(4, 3)
    gather_two.take(1)
    gather_two.send(6, 5)
    gather_two.take(4)
    gather_two.send(7)
    gather_two.take(6)
    gather_two.send(8)
    gather_two.take(2, 3, 5, 7, 8)
    part_two = toward(second)

    @pl.when(jnp.logical_and(is_even, leaf > 0))
    def _():
        tl_send[...] = part_two.astype(BF)
        tl_copy(leaf - 1).start()

    @pl.when(jnp.logical_not(is_even))
    def _():
        res[...] = srhs[...].astype(F32) - part_two

        @pl.when(leaf < n_leaf - 1)
        def _():
            tl_copy(leaf + 1).wait_recv()
            res[...] = res[...] - tl_recv[...].astype(F32)

        @pl.loop(0, level)
        def _(h):
            below = lax.shift_left(jnp.int32(1), h.astype(jnp.int32))
            for i in range(2):
                source = leaf + (1 - 2 * i) * below

                @pl.when(inside(source))
                def _():
                    up_copy(i, h, source).wait_recv()
                    res[...] = res[...] - up_recv[h, i].astype(F32)

        climb()

    loads[8].wait()
    solved_sep = nt(rb[...], sinv[...]).astype(BF).astype(F32)
    target_sep = (solved_sep + snoise[...].astype(F32)).astype(BF)
    zacc[...] = nn(target_sep, sinv[...])

    loads[9].wait()
    pack(n_buf, pkn)
    for step in range(1, n_front):
        exchange(pkn, rows_of(n2), nz_send, nz_recv, step).start()
    n2[:, own_rows, :] = pkn[front]

    for j in range(2):
        i = 1 - near if j == 0 else near
        source = ancestor(i)

        @pl.when(inside(source))
        def _():
            dn_copy(i, 0, source).wait_recv()
            zacc[...] = zacc[...] - nt(dn_recv[i], w[i])

    draws = zacc[...]
    sep_out[...] = draws
    dn_send[...] = draws.astype(BF)

    @pl.loop(0, level)
    def _(step):
        h = level - 1 - step
        below = lax.shift_left(jnp.int32(1), h.astype(jnp.int32))
        for i in range(2):
            target = leaf + (1 - 2 * i) * below

            @pl.when(inside(target))
            def _():
                dn_copy(i, h, target).start()

        for i in range(2):
            target = leaf + (1 - 2 * i) * below

            @pl.when(inside(target))
            def _():
                dn_copy(i, h, target).wait_send()

    @pl.when(is_even)
    def _():
        dn_copy(2, 0, leaf + 1).start()

    own_dup[0:HALF] = dn_send[...]
    own_dup[HALF:] = dn_send[...]

    def pulled(side, dup):
        return [
            jnp.where(low_lanes, nt(lw[side, t], dup), nt(lw[side, t + 2], dup)) for t in range(2)
        ]

    for t, value in enumerate(pulled(0, own_dup[...])):
        pull[t] = value
    for step in range(1, n_front):
        arrival(pkn, rows_of(n2), nz_send, nz_recv, step).wait_recv()

    @pl.when(jnp.logical_not(is_even))
    def _():
        dn_copy(2, 0, leaf - 1).wait_recv()
        prev_dup[0:HALF] = dn_recv[2]

    @pl.when(jnp.logical_and(is_even, leaf > 0))
    def _():
        prev_dup[0:HALF] = dn_recv[0]

    @pl.when(leaf == 0)
    def _():
        prev_dup[0:HALF] = jnp.zeros((HALF, prev_dup.shape[1]), BF)

    prev_dup[HALF:] = prev_dup[0:HALF]
    for t, value in enumerate(pulled(1, prev_dup[...])):
        mixed = s2[t].astype(F32) + n2[t].astype(F32) - pull[t] - value
        mixed = jnp.where(alive[t], mixed, 0.0).astype(BF)
        drawn = jnp.where(low_lanes, tn(inv[t], mixed), tn(inv[t + 2], mixed)).astype(BF)
        for f in range(n_front):
            d2[f, t] = drawn[f * rows : f * rows + rows]

    for step in range(1, n_front):
        exchange(d2, lambda f: o2.at[f], o_send, o_recv, step).start()
    o2[front] = d2[front]
    for step in range(1, n_front):
        arrival(d2, lambda f: o2.at[f], o_send, o_recv, step).wait_recv()

    for t in range(2):
        for slab in range(n_front // 2):
            lanes = slice(slab * 128, slab * 128 + 128)
            a = o2[2 * slab, t]
            b = o2[2 * slab + 1, t]
            leaf_out[t, :, lanes] = jnp.concatenate([a[:, :HALF], b[:, :HALF]], axis=1)
            leaf_out[t + 2, :, lanes] = jnp.concatenate([a[:, HALF:], b[:, HALF:]], axis=1)

    for step in range(1, n_front):
        exchange(pk, rows_of(r2), a_send, a_recv, step).wait_send()
        exchange(pkn, rows_of(n2), nz_send, nz_recv, step).wait_send()
        exchange(d2, lambda f: o2.at[f], o_send, o_recv, step).wait_send()
    gather_inv.drain()
    gather_one.drain()
    gather_two.drain()

    @pl.when(leaf > 0)
    def _():
        tl_copy(leaf - 1).wait_send()

    for i in range(2):
        target = ancestor(i)

        @pl.when(inside(target))
        def _():
            up_copy(i, own_level, target).wait_send()

    @pl.when(is_even)
    def _():
        dn_copy(2, 0, leaf + 1).wait_send()


def on_device(
    leaf_rhs,
    sep_rhs,
    leaf_noise,
    sep_noise,
    leaf_inverse,
    leaf_left,
    leaf_right,
    sep_inverse,
    sep_left,
    sep_right,
    leaf_count,
):
    n_leaf = lax.axis_size("leaf")
    n_front = lax.axis_size("front")
    depth = n_leaf.bit_length() - 1
    _, rows, slots, samples = leaf_rhs.shape
    share, width = sep_rhs.shape[1:]
    order = rows * n_front
    rhs = jnp.transpose(leaf_rhs[0], (1, 0, 2))
    noise = jnp.transpose(leaf_noise[0], (1, 0, 2))
    hbm = pl.BlockSpec(memory_space=pltpu.HBM)
    vmem = pl.BlockSpec(memory_space=pltpu.VMEM)
    dma = pltpu.SemaphoreType.DMA
    leaf_draws, sep_draws = pl.pallas_call(
        functools.partial(kernel, n_leaf, n_front, depth),
        out_shape=(
            jax.ShapeDtypeStruct((slots, rows, samples), BF),
            jax.ShapeDtypeStruct((share, width), F32),
        ),
        in_specs=[pl.BlockSpec(memory_space=pltpu.SMEM)] + [hbm] * 10,
        out_specs=(vmem, vmem),
        scratch_shapes=[
            pltpu.VMEM((slots, rows, samples), BF),
            pltpu.VMEM((slots, rows, samples), BF),
            pltpu.VMEM((n_front, 2, rows, 128), BF),
            pltpu.VMEM((n_front, 2, rows, 128), BF),
            pltpu.VMEM((2, order, 128), BF),
            pltpu.VMEM((2, order, 128), BF),
            pltpu.VMEM((slots, order, order), BF),
            pltpu.VMEM((2, slots, order, width), BF),
            pltpu.VMEM((share, width), BF),
            pltpu.VMEM((share, width), BF),
            pltpu.VMEM((width, width), BF),
            pltpu.VMEM((2, width, width), BF),
            pltpu.VMEM((2, width, width), BF),
            pltpu.VMEM((2, order, 128), BF),
            pltpu.VMEM((share, width), F32),
            pltpu.VMEM((share, width), BF),
            pltpu.VMEM((share, width), F32),
            pltpu.VMEM((share, width), BF),
            pltpu.VMEM((share, width), BF),
            pltpu.VMEM((2, share, width), BF),
            pltpu.VMEM((depth, 2, share, width), BF),
            pltpu.VMEM((share, width), BF),
            pltpu.VMEM((3, share, width), BF),
            pltpu.VMEM((2 * share, width), BF),
            pltpu.VMEM((2 * share, width), BF),
            pltpu.VMEM((2, order, 128), F32),
            pltpu.VMEM((n_front, 2, rows, 128), BF),
            pltpu.VMEM((n_front, 2, rows, 128), BF),
            dma((10,)),
            dma((n_front - 1,)),
            dma((n_front - 1,)),
            dma((n_front - 1,)),
            dma((n_front - 1,)),
            dma((9,)),
            dma((9,)),
            dma((2, 9)),
            dma((2, 9)),
            dma,
            dma,
            dma((2,)),
            dma((depth, 2)),
            dma((3, depth)),
            dma((3,)),
            dma((n_front - 1,)),
            dma((n_front - 1,)),
        ],
        compiler_params=pltpu.CompilerParams(
            collective_id=0, has_side_effects=True, vmem_limit_bytes=40 * 1024 * 1024
        ),
    )(
        leaf_count,
        rhs,
        noise,
        leaf_inverse[0],
        leaf_left[0],
        leaf_right[0],
        sep_rhs[0],
        sep_noise[0],
        sep_inverse[0],
        sep_left[0],
        sep_right[0],
    )
    leaf_draws = jnp.transpose(leaf_draws, (1, 0, 2)).astype(F32)
    return (leaf_draws[None], sep_draws[None])


def solution(mesh):
    return jax.shard_map(
        on_device,
        mesh=mesh,
        in_specs=(
            P("leaf", "front", None, None),
            P("leaf", "front", None),
            P("leaf", "front", None, None),
            P("leaf", "front", None),
            P("leaf", None, "front", None),
            P("leaf", None, "front", None),
            P("leaf", None, "front", None),
            P("leaf", None, None),
            P("leaf", None, None),
            P("leaf", None, None),
            P("leaf"),
        ),
        out_specs=(P("leaf", "front", None, None), P("leaf", "front", None)),
        check_vma=False,
    )
```

time: 455 us -> 135 us (0.30)
  waiting for transfers between devices: 237 us -> 0 us
  starting transfers between devices: 130 us -> 0 us
  Pallas kernels: 0 us -> 121 us
  matrix products: 53.1 us -> 0 us
  between operations: 15.6 us -> 1.31 us
  other arithmetic: 5.95 us -> 0.02 us
    ppermute x26 -> x0, starting transfers between devices: 130 us -> none  [shifted(): lax.ppermute(value, axis, [(source, source + steps) for source in range(f...]
    pallas_call x0 -> x1, Pallas kernels: none -> 121 us  [on_device(): pl.pallas_call(functools.partial(kernel, n_leaf, n_front, depth), out_sha...]
    all_gather x2 -> x0, waiting for transfers between devices: 94.6 us -> none  [the longest x1 56 us: on_device(): pull_shard_piece = lax.all_gather(stacked, 'front', axis=1, tiled=True)]
    unnamed x5 -> x0, waiting for transfers between devices: 74.5 us -> none
    dot_general x38 -> x0, matrix products: 53.1 us -> none  [the longest x7 16.6 us: on_device(): jnp.dot(combined.astype(jnp.bfloat16), sep_inv, preferred_element_type=jn...]
    reduce_scatter x1 -> x0, waiting for transfers between devices: 40.2 us -> none  [on_device(): lax.psum_scatter(jnp.concatenate([toward_right, toward_left], axis=1).ast...]
    ppermute x26 -> x0, waiting for transfers between devices: 27.4 us -> none  [shifted(): lax.ppermute(value, axis, [(source, source + steps) for source in range(f...]
    unnamed x46 -> x18, local copies, waits for them, and re-layouts: 4.92 us -> 9.83 us
  transfers between devices with their start and end apart: 30 -> 0, of which waited for: 21 -> 0; matrix products, arithmetic and copies ran while one was open for 2% -> 0% of each run, Pallas kernels for 0% -> 0%
where the time goes in v1:
time: 135 us; the launch traced here: 134 us
  Pallas kernels  121 us (90%)
  local copies, waits for them, and re-layouts  10.8 us (8%)
    pallas_call x1, Pallas kernels, on_device(): pl.pallas_call(functools.partial(kernel, n_leaf, n_front, depth), out_sha...  121 us
    unnamed x18, local copies, waits for them, and re-layouts  9.83 us

profile of v1, /device:TPU:1, one launch (start us, length us, event | category | flops | bytes accessed | tf_op | source)
XLA Modules:
  0.0 133.6 jit_solution(8348898919108848168)
XLA Ops:
  1.3 1.0 copy_bitcast_fusion
  2.3 0.0 copy-start
  2.3 1.3 copy-done
  3.6 0.0 copy-start.1
  3.6 1.3 copy-done.1
  4.8 0.0 copy-start.2
  4.8 1.3 copy-done.2
  6.1 0.0 copy-start.3
  6.1 0.9 copy-done.3
  7.0 0.0 copy-start.4
  7.0 0.9 copy-done.4
  8.0 0.0 copy-start.5
  8.0 0.9 copy-done.5
  8.9 0.0 copy-start.6
  8.9 0.9 copy-done.6
  9.8 0.0 copy-start.7
  9.8 0.8 copy-done.7
  10.6 121.4 %shard_map.122 = (bf16[4,32,512]{2,1,0:T(8,128)(2,1)S(1)}, f32[64,768]{1,0:T(8,128)S(1)}) custom-call(s32[1]{0:T(128)S(6)} %copy.19.cnt_ref, bf16[4,32,512]{2,1,0:T(8,128)(2,1)S(1)} %get-tuple-element.9.rhs_hbm, bf16[4,32,512]{2,1,0:T(8,128)(2,1)S(1)} %get-tuple-element.8.noise_hbm, bf16[4,32,256]{2,1,0:T(8,128)(2,1)S(1)} %bitcast.29, ...), custom_call_target="tpu_custom_call" | custom-call | tf_op jit(solution)/shard_map/pallas_call | solution.py:555
  132.0 0.9 copy.15
  132.9 0.7 copy.20
  (1 shorter events, 0.0 us)
Async XLA Ops:
  2.3 1.3 copy-start
  3.6 1.3 copy-start.1
  4.8 1.3 copy-start.2
  6.1 0.9 copy-start.3
  7.0 0.9 copy-start.4
  8.0 0.9 copy-start.5
  8.9 0.9 copy-start.6
  9.8 0.8 copy-start.7

commit v2 on v1

--- a/solution.py
+++ b/solution.py
@@ -11,6 +11,7 @@
 BF = jnp.bfloat16
 F32 = jnp.float32
 HALF = 64
+SKIPPED = (3, 5)
 
 
 def nn(a, b):
@@ -66,7 +67,8 @@
     snoise,
     sinv,
     su,
-    w,
+    wall,
+    wa,
     s2,
     res,
     rb,
@@ -77,6 +79,8 @@
     up_recv,
     dn_send,
     dn_recv,
+    zp_send,
+    zp_recv,
     own_dup,
     prev_dup,
     pull,
@@ -99,6 +103,13 @@
     dn_rsem,
     o_send,
     o_recv,
+    wa_ssem,
+    wa_rsem,
+    cx_ssem,
+    cx_rsem,
+    zp_ssem,
+    zp_rsem,
+    known_sem,
 ):
     leaf = lax.axis_index("leaf")
     front = lax.axis_index("front")
@@ -119,6 +130,28 @@
     def inside(target):
         return jnp.logical_and(target >= 0, target < n_leaf)
 
+    def any_of(value, levels):
+        found = jnp.bool_(False)
+        for one in levels:
+            found = jnp.logical_or(found, value == one)
+        return found
+
+    skipped = tuple(one for one in SKIPPED if one < depth)
+    is_skipped = any_of(level, skipped)
+    is_joined = any_of(level + 1, skipped)
+    joined = is_joined.astype(jnp.int32)
+    near = ((pos // span) % 4 == 1).astype(jnp.int32)
+    parent = leaf + (2 * near - 1) * span
+    parent_near = (((parent + 1) // (2 * span)) % 4 == 1).astype(jnp.int32)
+    first_side = jnp.where(is_joined, parent_near, near)
+    own_level = jnp.minimum(level, depth - 1)
+    half_span = jnp.maximum(span // 2, 1)
+
+    def ancestor(i):
+        reach = jnp.where(jnp.logical_and(is_joined, near == i), 3, 1)
+        return leaf + (2 * i - 1) * reach * span
+
+
     def load(i, src, dst):
         return pltpu.make_async_copy(src, dst, load_sem.at[i])
 
@@ -144,19 +177,63 @@
         pl.semaphore_signal(
             barrier, inc=1, device_id={"front": (front + step) % n_front}, device_id_type=MESH
         )
-    for h in range(depth + 1):
-        for sign in (-1, 1):
-            target = leaf + sign * (1 << h)
-            reached = jnp.logical_and(h <= level, inside(target))
-            partners = partners + reached.astype(jnp.int32)
-
-            @pl.when(reached)
-            def _():
-                pl.semaphore_signal(
-                    barrier, inc=1, device_id={"leaf": target}, device_id_type=MESH
+    greeted = [(leaf - 1, leaf > 0), (leaf + 1, leaf < n_leaf - 1)]
+    if skipped:
+        greeted += [
+            (parent, is_joined),
+            (leaf - half_span, is_skipped),
+            (leaf + half_span, is_skipped),
+            (ancestor(0), jnp.logical_and(is_joined, inside(ancestor(0)))),
+            (ancestor(1), jnp.logical_and(is_joined, inside(ancestor(1)))),
+        ]
+        for one in skipped:
+            for reach in (-3 << (one - 1), -1 << (one - 1), 1 << (one - 1), 3 << (one - 1)):
+                greeted.append(
+                    (leaf + reach, jnp.logical_and(level > one, inside(leaf + reach)))
                 )
-
+    for target, reached in greeted:
+        partners = partners + reached.astype(jnp.int32)
+
+        @pl.when(reached)
+        def _():
+            pl.semaphore_signal(barrier, inc=1, device_id={"leaf": target}, device_id_type=MESH)
+
+    loads[0].wait()
+    pack(x_buf, pk)
+    loads[4].wait()
+    loads[5].wait()
+    wall[0] = tn(sinv[...], su[0]).astype(BF)
     pl.semaphore_wait(barrier, partners)
+
+    width = srhs.shape[1]
+    cols = pl.ds(pl.multiple_of(core * (width // 2), 128), width // 2)
+
+    def wa_copy(i, target):
+        return pltpu.make_async_remote_copy(
+            src_ref=wall.at[0:2, :, cols],
+            dst_ref=wa.at[:, :, cols],
+            send_sem=wa_ssem.at[i],
+            recv_sem=wa_rsem,
+            device_id={"leaf": target},
+            device_id_type=MESH,
+        )
+
+    def cx_copy(which):
+        half = pl.ds(pl.multiple_of(which * (width // 2), 128), width // 2)
+        return pltpu.make_async_remote_copy(
+            src_ref=wall.at[2:4, :, half],
+            dst_ref=wall.at[2:4, :, half],
+            send_sem=cx_ssem,
+            recv_sem=cx_rsem,
+            device_id={"front": 2 * x + 1 - core},
+            device_id_type=MESH,
+        )
+
+    if skipped:
+
+        @pl.when(is_joined)
+        def _():
+            pl.semaphore_signal(known_sem, inc=1, device_id={"leaf": parent}, device_id_type=MESH)
 
     def exchange(src, dst_at, sends, recvs, step):
         peer = (front + step) % n_front
@@ -250,8 +327,6 @@
     gather_one = Gather(lw.at[first], g_send.at[0], g_recv.at[0])
     gather_two = Gather(lw.at[second], g_send.at[1], g_recv.at[1])
 
-    loads[0].wait()
-    pack(x_buf, pk)
     for step in range(1, n_front):
         exchange(pk, rows_of(r2), a_send, a_recv, step).start()
     loads[1].wait()
@@ -261,15 +336,19 @@
     gather_one.send(0, 1, 2)
     r2[:, own_rows, :] = pk[front]
 
-    loads[4].wait()
-    loads[5].wait()
-    w[0] = tn(sinv[...], su[0]).astype(BF)
+    loads[6].wait()
+    wall[1] = tn(sinv[...], su[1]).astype(BF)
+    if skipped:
+
+        @pl.when(is_skipped)
+        def _():
+            for i in range(2):
+                wa_copy(i, leaf + (1 - 2 * i) * half_span).start()
+
     gather_inv.take(0)
     gather_inv.send(4, 3)
     gather_inv.take(1)
     gather_inv.send(6, 5)
-    loads[6].wait()
-    w[1] = tn(sinv[...], su[1]).astype(BF)
     gather_one.take(0)
     gather_one.send(4, 3)
     gather_one.take(1)
@@ -315,42 +394,87 @@
             device_id_type=MESH,
         )
 
-    def up_copy(i, h, target):
-        return pltpu.make_async_remote_copy(
-            src_ref=up_send.at[i],
-            dst_ref=up_recv.at[h, i],
-            send_sem=up_ssem.at[i],
-            recv_sem=up_rsem.at[h, i],
-            device_id={"leaf": target},
-            device_id_type=MESH,
-        )
-
-    def dn_copy(i, h, target):
-        return pltpu.make_async_remote_copy(
-            src_ref=dn_send,
-            dst_ref=dn_recv.at[i],
-            send_sem=dn_ssem.at[i, h],
-            recv_sem=dn_rsem.at[i],
-            device_id={"leaf": target},
-            device_id_type=MESH,
-        )
-
-    near = ((pos // span) % 4 == 1).astype(jnp.int32)
-    own_level = jnp.minimum(level, depth - 1)
-
-    def ancestor(i):
-        return leaf + (2 * i - 1) * span
+    chunks = [(0, 256), (256, width)] if width > 256 else [(0, width)]
+
+    class Message:
+        def __init__(self, src, dst, sends, recvs, target):
+            self.parts = [
+                pltpu.make_async_remote_copy(
+                    src_ref=src.at[:, low:high],
+                    dst_ref=dst.at[:, low:high],
+                    send_sem=sends.at[n],
+                    recv_sem=recvs.at[n],
+                    device_id={"leaf": target},
+                    device_id_type=MESH,
+                )
+                for n, (low, high) in enumerate(chunks)
+            ]
+
+        def start(self):
+            for part in self.parts:
+                part.start()
+
+        def wait_send(self):
+            for part in self.parts:
+                part.wait_send()
+
+        def wait_recv(self):
+            for part in self.parts:
+                part.wait_recv()
+
+    def up_message(buffer, i, far, h, target):
+        return Message(
+            up_send.at[buffer],
+            up_recv.at[far, h, i],
+            up_ssem.at[buffer],
+            up_rsem.at[far, h, i],
+            target,
+        )
+
+    def dn_message(i, far, h, target):
+        return Message(dn_send, dn_recv.at[i], dn_ssem.at[far, i, h], dn_rsem.at[i], target)
+
+    def zp_message(i, target):
+        return Message(zp_send, zp_recv, zp_ssem.at[i], zp_rsem, target)
+
+    def post(buffer, matrix, message):
+        for n, (low, high) in enumerate(chunks):
+            up_send[buffer, :, low:high] = nn(rb[...], wall[matrix, :, low:high]).astype(BF)
+            message.parts[n].start()
+
+    def far_of(i):
+        return jnp.logical_and(is_joined, near == i).astype(jnp.int32)
 
     def climb():
         rb[...] = res[...].astype(BF)
         for j in range(2):
-            i = near if j == 0 else 1 - near
+            i = first_side if j == 0 else 1 - first_side
             target = ancestor(i)
 
             @pl.when(inside(target))
             def _():
-                up_send[i] = nn(rb[...], w[i]).astype(BF)
-                up_copy(i, own_level, target).start()
+                post(i, i + 2 * joined, up_message(i, i, far_of(i), own_level, target))
+
+    def gather_level(h):
+        below = lax.shift_left(jnp.int32(1), jnp.int32(h))
+        ahead = any_of(jnp.int32(h) + 1, skipped)
+        for i in range(2):
+            source = leaf + (1 - 2 * i) * below
+
+            @pl.when(inside(source))
+            def _():
+                up_message(i, i, 0, h, source).wait_recv()
+                res[...] = res[...] - up_recv[0, h, i].astype(F32)
+
+            if skipped:
+                source3 = leaf + (1 - 2 * i) * 3 * below
+
+                @pl.when(
+                    jnp.logical_and(jnp.logical_and(ahead, level > h + 1), inside(source3))
+                )
+                def _():
+                    up_message(i, i, 1, h, source3).wait_recv()
+                    res[...] = res[...] - up_recv[1, h, i].astype(F32)
 
     gather_one.take(4)
     gather_one.send(7)
@@ -360,6 +484,16 @@
     loads[7].wait()
     part_one = toward(first)
 
+    @pl.when(jnp.logical_not(is_even))
+    def _():
+        tl_send[...] = part_one.astype(BF)
+        tl_copy(leaf - 1).start()
+
+    gather_two.take(0)
+    gather_two.send(4, 3)
+    gather_two.take(1)
+    gather_two.send(6, 5)
+
     @pl.when(is_even)
     def _():
         res[...] = srhs[...].astype(F32) - part_one
@@ -367,15 +501,6 @@
         res[...] = res[...] - tl_recv[...].astype(F32)
         climb()
 
-    @pl.when(jnp.logical_not(is_even))
-    def _():
-        tl_send[...] = part_one.astype(BF)
-        tl_copy(leaf - 1).start()
-
-    gather_two.take(0)
-    gather_two.send(4, 3)
-    gather_two.take(1)
-    gather_two.send(6, 5)
     gather_two.take(4)
     gather_two.send(7)
     gather_two.take(6)
@@ -397,23 +522,52 @@
             tl_copy(leaf + 1).wait_recv()
             res[...] = res[...] - tl_recv[...].astype(F32)
 
-        @pl.loop(0, level)
+        if skipped:
+
+            @pl.when(is_joined)
+            def _():
+                wa_copy(0, parent).wait_recv()
+                turn = wall[near]
+                wall[2 + near, :, cols] = (-nn(turn, wa[near, :, cols])).astype(BF)
+                wall[3 - near, :, cols] = (
+                    wall[1 - near, :, cols].astype(F32) - nn(turn, wa[1 - near, :, cols])
+                ).astype(BF)
+                cx_copy(core).start()
+                cx_copy(1 - core).wait_recv()
+
+        @pl.loop(0, level - is_skipped.astype(jnp.int32))
         def _(h):
-            below = lax.shift_left(jnp.int32(1), h.astype(jnp.int32))
-            for i in range(2):
-                source = leaf + (1 - 2 * i) * below
-
-                @pl.when(inside(source))
-                def _():
-                    up_copy(i, h, source).wait_recv()
-                    res[...] = res[...] - up_recv[h, i].astype(F32)
+            gather_level(h)
+
+        if skipped:
+
+            @pl.when(is_skipped)
+            def _():
+                pl.semaphore_wait(known_sem, 2)
 
         climb()
+        if skipped:
+
+            @pl.when(is_joined)
+            def _():
+                post(2, near, up_message(2, near, 0, own_level, parent))
+
+            @pl.when(is_skipped)
+            def _():
+                gather_level(level - 1)
+                rb[...] = res[...].astype(BF)
 
     loads[8].wait()
     solved_sep = nt(rb[...], sinv[...]).astype(BF).astype(F32)
     target_sep = (solved_sep + snoise[...].astype(F32)).astype(BF)
     zacc[...] = nn(target_sep, sinv[...])
+    if skipped:
+
+        @pl.when(is_skipped)
+        def _():
+            zp_send[...] = zacc[...].astype(BF)
+            for i in range(2):
+                zp_message(i, leaf + (1 - 2 * i) * half_span).start()
 
     loads[9].wait()
     pack(n_buf, pkn)
@@ -421,40 +575,54 @@
         exchange(pkn, rows_of(n2), nz_send, nz_recv, step).start()
     n2[:, own_rows, :] = pkn[front]
 
+    if skipped:
+
+        @pl.when(is_joined)
+        def _():
+            zp_message(0, parent).wait_recv()
+            zacc[...] = zacc[...] - nt(zp_recv[...], wall[near])
+
     for j in range(2):
-        i = 1 - near if j == 0 else near
+        i = 1 - first_side if j == 0 else first_side
         source = ancestor(i)
 
         @pl.when(inside(source))
         def _():
-            dn_copy(i, 0, source).wait_recv()
-            zacc[...] = zacc[...] - nt(dn_recv[i], w[i])
+            dn_message(i, 0, 0, source).wait_recv()
+            zacc[...] = zacc[...] - nt(dn_recv[i], wall[i + 2 * joined])
 
     draws = zacc[...]
     sep_out[...] = draws
     dn_send[...] = draws.astype(BF)
 
+    def for_level(h, act):
+        below = lax.shift_left(jnp.int32(1), jnp.int32(h))
+        ahead = any_of(jnp.int32(h) + 1, skipped)
+        for i in range(2):
+            target = leaf + (1 - 2 * i) * below
+            target3 = leaf + (1 - 2 * i) * 3 * below
+            passed = jnp.logical_and(ahead, level == h + 1)
+
+            @pl.when(jnp.logical_and(jnp.logical_not(passed), inside(target)))
+            def _():
+                act(dn_message(i, 0, h, target))
+
+            if skipped:
+
+                @pl.when(
+                    jnp.logical_and(jnp.logical_and(ahead, level > h + 1), inside(target3))
+                )
+                def _():
+                    act(dn_message(i, 1, h, target3))
+
     @pl.loop(0, level)
     def _(step):
-        h = level - 1 - step
-        below = lax.shift_left(jnp.int32(1), h.astype(jnp.int32))
-        for i in range(2):
-            target = leaf + (1 - 2 * i) * below
-
-            @pl.when(inside(target))
-            def _():
-                dn_copy(i, h, target).start()
-
-        for i in range(2):
-            target = leaf + (1 - 2 * i) * below
-
-            @pl.when(inside(target))
-            def _():
-                dn_copy(i, h, target).wait_send()
+        for_level(level - 1 - step, lambda message: message.start())
+        for_level(level - 1 - step, lambda message: message.wait_send())
 
     @pl.when(is_even)
     def _():
-        dn_copy(2, 0, leaf + 1).start()
+        dn_message(2, 0, 0, leaf + 1).start()
 
     own_dup[0:HALF] = dn_send[...]
     own_dup[HALF:] = dn_send[...]
@@ -471,7 +639,7 @@
 
     @pl.when(jnp.logical_not(is_even))
     def _():
-        dn_copy(2, 0, leaf - 1).wait_recv()
+        dn_message(2, 0, 0, leaf - 1).wait_recv()
         prev_dup[0:HALF] = dn_recv[2]
 
     @pl.when(jnp.logical_and(is_even, leaf > 0))
@@ -521,11 +689,25 @@
 
         @pl.when(inside(target))
         def _():
-            up_copy(i, own_level, target).wait_send()
+            up_message(i, i, far_of(i), own_level, target).wait_send()
 
     @pl.when(is_even)
     def _():
-        dn_copy(2, 0, leaf + 1).wait_send()
+        dn_message(2, 0, 0, leaf + 1).wait_send()
+
+    if skipped:
+
+        @pl.when(is_joined)
+        def _():
+            up_message(2, near, 0, own_level, parent).wait_send()
+            cx_copy(core).wait_send()
+
+        @pl.when(is_skipped)
+        def _():
+            for i in range(2):
+                child = leaf + (1 - 2 * i) * half_span
+                wa_copy(i, child).wait_send()
+                zp_message(i, child).wait_send()
 
 
 def on_device(
@@ -573,6 +755,7 @@
             pltpu.VMEM((share, width), BF),
             pltpu.VMEM((width, width), BF),
             pltpu.VMEM((2, width, width), BF),
+            pltpu.VMEM((4, width, width), BF),
             pltpu.VMEM((2, width, width), BF),
             pltpu.VMEM((2, order, 128), BF),
             pltpu.VMEM((share, width), F32),
@@ -580,10 +763,12 @@
             pltpu.VMEM((share, width), F32),
             pltpu.VMEM((share, width), BF),
             pltpu.VMEM((share, width), BF),
-            pltpu.VMEM((2, share, width), BF),
-            pltpu.VMEM((depth, 2, share, width), BF),
+            pltpu.VMEM((3, share, width), BF),
+            pltpu.VMEM((2, depth, 2, share, width), BF),
             pltpu.VMEM((share, width), BF),
             pltpu.VMEM((3, share, width), BF),
+            pltpu.VMEM((share, width), BF),
+            pltpu.VMEM((share, width), BF),
             pltpu.VMEM((2 * share, width), BF),
             pltpu.VMEM((2 * share, width), BF),
             pltpu.VMEM((2, order, 128), F32),
@@ -600,15 +785,22 @@
             dma((2, 9)),
             dma,
             dma,
-            dma((2,)),
-            dma((depth, 2)),
-            dma((3, depth)),
-            dma((3,)),
+            dma((3, 2)),
+            dma((2, depth, 2, 2)),
+            dma((2, 3, depth, 2)),
+            dma((3, 2)),
             dma((n_front - 1,)),
             dma((n_front - 1,)),
+            dma((2,)),
+            dma,
+            dma,
+            dma,
+            dma((2, 2)),
+            dma((2,)),
+            pltpu.SemaphoreType.REGULAR,
         ],
         compiler_params=pltpu.CompilerParams(
-            collective_id=0, has_side_effects=True, vmem_limit_bytes=40 * 1024 * 1024
+            collective_id=0, has_side_effects=True, vmem_limit_bytes=63 * 1024 * 1024
         ),
     )(
         leaf_count,

time: 135 us -> 124 us (0.919)
  local copies, waits for them, and re-layouts: 10.8 us -> 4.2 us
  Pallas kernels: 121 us -> 116 us
    unnamed x18 -> x2, local copies, waits for them, and re-layouts: 9.83 us -> 2.49 us
    pallas_call x1, Pallas kernels: 121 us -> 116 us  [on_device(): pl.pallas_call(functools.partial(kernel, n_leaf, n_front, depth), out_sha...]
where the time goes in v2:
time: 124 us; the launch traced here: 122 us
  Pallas kernels  116 us (94%)
  local copies, waits for them, and re-layouts  4.2 us (3%)
  between operations  1.29 us (1%)
    pallas_call x1, Pallas kernels, on_device(): pl.pallas_call(functools.partial(kernel, n_leaf, n_front, depth), out_sha...  116 us
    unnamed x2, local copies, waits for them, and re-layouts  2.49 us

profile of v2, /device:TPU:1, one launch (start us, length us, event | category | flops | bytes accessed | tf_op | source)
XLA Modules:
  0.0 122.4 jit_solution(384203904761576444)
XLA Ops:
  1.3 1.7 %copy_bitcast_fusion = (bf16[4,32,512]{2,1,0:T(8,128)(2,1)}, bf16[4,32,512]{2,1,0:T(8,128)(2,1)}) fusion(bf16[1,32,4,512]{3,2,1,0:T(4,128)(2,1)} %param.13, bf16[1,32,4,512]{3,2,1,0:T(4,128)(2,1)} %param.11), kind=kLoop, calls=%fused_computation.1 | loop fusion | bytes 524288 | tf_op jit(solution)/shard_map/transpose | solution.py:733
  3.0 116.0 %shard_map.122 = (bf16[4,32,512]{2,1,0:T(8,128)(2,1)}, f32[64,768]{1,0:T(8,128)}) custom-call(s32[1]{0:T(128)S(6)} %copy.19.cnt_ref, bf16[4,32,512]{2,1,0:T(8,128)(2,1)} %get-tuple-element.9.rhs_hbm, bf16[4,32,512]{2,1,0:T(8,128)(2,1)} %get-tuple-element.8.noise_hbm, bf16[4,32,256]{2,1,0:T(8,128)(2,1)} %bitcast.29, bf16[4,32,768]{2,1,0:T(8,128)(2,1)} %bitcast.24, ...), custom_call_target="tpu_custom_call" | custom-call | tf_op jit(solution)/shard_map/pallas_call | solution.py:737
  119.0 0.9 convert_bitcast_fusion
  119.9 0.9 copy.15
  120.8 1.6 %copy.20 = f32[1,64,768]{2,1,0:T(8,128)} copy(f32[1,64,768]{2,1,0:T(8,128)} %bitcast.26) | data formatting | bytes 393216

commit v3 on v2

--- a/solution.py
+++ b/solution.py
@@ -68,7 +68,7 @@
     sinv,
     su,
     wall,
-    wa,
+    hw,
     s2,
     res,
     rb,
@@ -81,6 +81,10 @@
     dn_recv,
     zp_send,
     zp_recv,
+    hu_recv,
+    v_send,
+    dv_recv,
+    da,
     own_dup,
     prev_dup,
     pull,
@@ -103,10 +107,15 @@
     dn_rsem,
     o_send,
     o_recv,
-    wa_ssem,
-    wa_rsem,
-    cx_ssem,
-    cx_rsem,
+    hw_ssem,
+    hw_rsem,
+    gh_send,
+    gh_recv,
+    hu_ssem,
+    hu_rsem,
+    v_ssem,
+    dv_rsem,
+    da_ssem,
     zp_ssem,
     zp_rsem,
     known_sem,
@@ -142,15 +151,41 @@
     joined = is_joined.astype(jnp.int32)
     near = ((pos // span) % 4 == 1).astype(jnp.int32)
     parent = leaf + (2 * near - 1) * span
-    parent_near = (((parent + 1) // (2 * span)) % 4 == 1).astype(jnp.int32)
-    first_side = jnp.where(is_joined, parent_near, near)
     own_level = jnp.minimum(level, depth - 1)
     half_span = jnp.maximum(span // 2, 1)
+    lowest = skipped[0] if skipped else depth
+    is_host = level > lowest
+    is_top = leaf == n_leaf - 1
+    top_hosts_two = len(skipped) == 2
 
     def ancestor(i):
-        reach = jnp.where(jnp.logical_and(is_joined, near == i), 3, 1)
-        return leaf + (2 * i - 1) * reach * span
-
+        return leaf + (2 * i - 1) * span
+
+    def group_host(i):
+        return jnp.where(is_skipped, ancestor(i), parent + (2 * i - 1) * 2 * span)
+
+    def host_slot(i):
+        far_group = jnp.logical_or(level == skipped[-1], level + 1 == skipped[-1])
+        return jnp.where(jnp.logical_and(far_group, top_hosts_two), 1, 1 - i)
+
+    def group_of(slot):
+        if slot == 0:
+            return leaf - (1 << lowest), jnp.int32(1 << (lowest - 1))
+        if top_hosts_two:
+            other = 1 << skipped[-1]
+            return (
+                jnp.where(is_top, leaf - other, leaf + (1 << lowest)),
+                jnp.where(is_top, jnp.int32(other // 2), jnp.int32(1 << (lowest - 1))),
+            )
+        return leaf + (1 << lowest), jnp.int32(1 << (lowest - 1))
+
+    def group_side(slot):
+        if slot == 0:
+            return jnp.int32(1)
+        return is_top.astype(jnp.int32)
+
+    def has_group(slot):
+        return jnp.logical_and(is_host, inside(group_of(slot)[0]))
 
     def load(i, src, dst):
         return pltpu.make_async_copy(src, dst, load_sem.at[i])
@@ -183,14 +218,12 @@
             (parent, is_joined),
             (leaf - half_span, is_skipped),
             (leaf + half_span, is_skipped),
-            (ancestor(0), jnp.logical_and(is_joined, inside(ancestor(0)))),
-            (ancestor(1), jnp.logical_and(is_joined, inside(ancestor(1)))),
+            (group_host(0), jnp.logical_and(is_joined, inside(group_host(0)))),
+            (group_host(1), jnp.logical_and(is_joined, inside(group_host(1)))),
         ]
-        for one in skipped:
-            for reach in (-3 << (one - 1), -1 << (one - 1), 1 << (one - 1), 3 << (one - 1)):
-                greeted.append(
-                    (leaf + reach, jnp.logical_and(level > one, inside(leaf + reach)))
-                )
+        for slot in range(2):
+            center, reach = group_of(slot)
+            greeted += [(center - reach, has_group(slot)), (center + reach, has_group(slot))]
     for target, reached in greeted:
         partners = partners + reached.astype(jnp.int32)
 
@@ -206,26 +239,16 @@
     pl.semaphore_wait(barrier, partners)
 
     width = srhs.shape[1]
-    cols = pl.ds(pl.multiple_of(core * (width // 2), 128), width // 2)
-
-    def wa_copy(i, target):
+    share_rows = width // n_front
+    share_here = pl.ds(pl.multiple_of(front * share_rows, share_rows), share_rows)
+
+    def hw_copy(i, slot, target):
         return pltpu.make_async_remote_copy(
-            src_ref=wall.at[0:2, :, cols],
-            dst_ref=wa.at[:, :, cols],
-            send_sem=wa_ssem.at[i],
-            recv_sem=wa_rsem,
+            src_ref=wall.at[i, share_here],
+            dst_ref=hw.at[slot, share_here],
+            send_sem=hw_ssem.at[i],
+            recv_sem=hw_rsem.at[slot],
             device_id={"leaf": target},
-            device_id_type=MESH,
-        )
-
-    def cx_copy(which):
-        half = pl.ds(pl.multiple_of(which * (width // 2), 128), width // 2)
-        return pltpu.make_async_remote_copy(
-            src_ref=wall.at[2:4, :, half],
-            dst_ref=wall.at[2:4, :, half],
-            send_sem=cx_ssem,
-            recv_sem=cx_rsem,
-            device_id={"front": 2 * x + 1 - core},
             device_id_type=MESH,
         )
 
@@ -263,7 +286,10 @@
     def piece(buf, dx, flip, low, high):
         chip = (x + dx + chips) % chips
         who = 2 * chip + (1 - core if flip else core)
-        return buf.at[low:high, pl.ds(pl.multiple_of(who * rows, rows), rows), :]
+        count, order, _ = buf.shape
+        low, high = low * count // 4, high * count // 4
+        some = order // n_front
+        return buf.at[low:high, pl.ds(pl.multiple_of(who * some, some), some), :]
 
     routes = [
         (0, 0, 4, 1, False),
@@ -324,6 +350,7 @@
     first = odd
     second = 1 - odd
     gather_inv = Gather(inv, gi_send, gi_recv)
+    gather_host = Gather(hw, gh_send, gh_recv)
     gather_one = Gather(lw.at[first], g_send.at[0], g_recv.at[0])
     gather_two = Gather(lw.at[second], g_send.at[1], g_recv.at[1])
 
@@ -338,17 +365,21 @@
 
     loads[6].wait()
     wall[1] = tn(sinv[...], su[1]).astype(BF)
-    if skipped:
-
-        @pl.when(is_skipped)
-        def _():
-            for i in range(2):
-                wa_copy(i, leaf + (1 - 2 * i) * half_span).start()
-
     gather_inv.take(0)
     gather_inv.send(4, 3)
     gather_inv.take(1)
     gather_inv.send(6, 5)
+    if skipped:
+
+        @pl.when(is_skipped)
+        def _():
+            pl.semaphore_wait(known_sem, 2)
+            for i in range(2):
+
+                @pl.when(inside(ancestor(i)))
+                def _():
+                    hw_copy(i, host_slot(i), ancestor(i)).start()
+
     gather_one.take(0)
     gather_one.send(4, 3)
     gather_one.take(1)
@@ -422,59 +453,65 @@
             for part in self.parts:
                 part.wait_recv()
 
-    def up_message(buffer, i, far, h, target):
+    def up_message(i, h, target):
+        return Message(up_send.at[i], up_recv.at[h, i], up_ssem.at[i], up_rsem.at[h, i], target)
+
+    def hu_message(i, slot, which, target):
         return Message(
-            up_send.at[buffer],
-            up_recv.at[far, h, i],
-            up_ssem.at[buffer],
-            up_rsem.at[far, h, i],
-            target,
-        )
-
-    def dn_message(i, far, h, target):
-        return Message(dn_send, dn_recv.at[i], dn_ssem.at[far, i, h], dn_rsem.at[i], target)
+            up_send.at[near], hu_recv.at[slot, which], hu_ssem.at[i], hu_rsem.at[slot, which], target
+        )
+
+    def dn_message(i, h, target):
+        return Message(dn_send, dn_recv.at[i], dn_ssem.at[i, h], dn_rsem.at[i], target)
+
+    def v_message(slot, which, side, target):
+        return Message(
+            v_send.at[slot], dv_recv.at[side], v_ssem.at[slot, which], dv_rsem.at[side], target
+        )
+
+    def da_message(target):
+        return Message(da, dn_recv.at[near], da_ssem, dn_rsem.at[near], target)
 
     def zp_message(i, target):
         return Message(zp_send, zp_recv, zp_ssem.at[i], zp_rsem, target)
-
-    def post(buffer, matrix, message):
-        for n, (low, high) in enumerate(chunks):
-            up_send[buffer, :, low:high] = nn(rb[...], wall[matrix, :, low:high]).astype(BF)
-            message.parts[n].start()
-
-    def far_of(i):
-        return jnp.logical_and(is_joined, near == i).astype(jnp.int32)
 
     def climb():
         rb[...] = res[...].astype(BF)
         for j in range(2):
-            i = first_side if j == 0 else 1 - first_side
+            i = near if j == 0 else 1 - near
             target = ancestor(i)
 
             @pl.when(inside(target))
             def _():
-                post(i, i + 2 * joined, up_message(i, i, far_of(i), own_level, target))
+                message = up_message(i, own_level, target)
+                for n, (low, high) in enumerate(chunks):
+                    up_send[i, :, low:high] = nn(rb[...], wall[i, :, low:high]).astype(BF)
+                    if j == 1 or not skipped:
+                        message.parts[n].start()
+                    else:
+
+                        @pl.when(is_joined)
+                        def _():
+                            for side in range(2):
+
+                                @pl.when(inside(group_host(side)))
+                                def _():
+                                    to_host(side).parts[n].start()
+
+                        message.parts[n].start()
+
+    def to_host(side):
+        return hu_message(side, host_slot(side), 1 - near, group_host(side))
 
     def gather_level(h):
         below = lax.shift_left(jnp.int32(1), jnp.int32(h))
-        ahead = any_of(jnp.int32(h) + 1, skipped)
         for i in range(2):
             source = leaf + (1 - 2 * i) * below
 
             @pl.when(inside(source))
             def _():
-                up_message(i, i, 0, h, source).wait_recv()
-                res[...] = res[...] - up_recv[0, h, i].astype(F32)
-
-            if skipped:
-                source3 = leaf + (1 - 2 * i) * 3 * below
-
-                @pl.when(
-                    jnp.logical_and(jnp.logical_and(ahead, level > h + 1), inside(source3))
-                )
-                def _():
-                    up_message(i, i, 1, h, source3).wait_recv()
-                    res[...] = res[...] - up_recv[1, h, i].astype(F32)
+                up_message(i, h, source).wait_recv()
+                res[...] = res[...] - up_recv[h, i].astype(F32)
 
     gather_one.take(4)
     gather_one.send(7)
@@ -524,16 +561,23 @@
 
         if skipped:
 
-            @pl.when(is_joined)
-            def _():
-                wa_copy(0, parent).wait_recv()
-                turn = wall[near]
-                wall[2 + near, :, cols] = (-nn(turn, wa[near, :, cols])).astype(BF)
-                wall[3 - near, :, cols] = (
-                    wall[1 - near, :, cols].astype(F32) - nn(turn, wa[1 - near, :, cols])
-                ).astype(BF)
-                cx_copy(core).start()
-                cx_copy(1 - core).wait_recv()
+            @pl.when(is_host)
+            def _():
+                for slot in range(2):
+
+                    @pl.when(has_group(slot))
+                    def _():
+                        hw_copy(0, slot, group_of(slot)[0]).wait_recv()
+
+                gather_host.send(0, 1, 2)
+                gather_host.take(0)
+                gather_host.send(4, 3)
+                gather_host.take(1)
+                gather_host.send(6, 5)
+                gather_host.take(4)
+                gather_host.send(7)
+                gather_host.take(6)
+                gather_host.send(8)
 
         @pl.loop(0, level - is_skipped.astype(jnp.int32))
         def _(h):
@@ -541,16 +585,21 @@
 
         if skipped:
 
-            @pl.when(is_skipped)
-            def _():
-                pl.semaphore_wait(known_sem, 2)
+            @pl.when(is_host)
+            def _():
+                gather_host.take(2, 3, 5, 7, 8)
+                for slot in range(2):
+
+                    @pl.when(has_group(slot))
+                    def _():
+                        center, reach = group_of(slot)
+                        hu_message(0, slot, 0, center - reach).wait_recv()
+                        hu_message(0, slot, 1, center + reach).wait_recv()
+                        both = hu_recv[slot, 0].astype(F32) + hu_recv[slot, 1].astype(F32)
+                        res[...] = res[...] + nn(both.astype(BF), hw[slot])
 
         climb()
         if skipped:
-
-            @pl.when(is_joined)
-            def _():
-                post(2, near, up_message(2, near, 0, own_level, parent))
 
             @pl.when(is_skipped)
             def _():
@@ -575,21 +624,46 @@
         exchange(pkn, rows_of(n2), nz_send, nz_recv, step).start()
     n2[:, own_rows, :] = pkn[front]
 
+    is_plain = jnp.logical_not(jnp.logical_or(is_skipped, is_joined))
+
+    def take_draws(i, wanted):
+        source = ancestor(i)
+
+        @pl.when(jnp.logical_and(wanted, inside(source)))
+        def _():
+            dn_message(i, 0, source).wait_recv()
+            zacc[...] = zacc[...] - nt(dn_recv[i], wall[i])
+
+    take_draws(1 - near, jnp.logical_not(is_skipped))
+    take_draws(near, is_plain)
     if skipped:
 
         @pl.when(is_joined)
         def _():
             zp_message(0, parent).wait_recv()
-            zacc[...] = zacc[...] - nt(zp_recv[...], wall[near])
-
-    for j in range(2):
-        i = 1 - first_side if j == 0 else first_side
-        source = ancestor(i)
-
-        @pl.when(inside(source))
-        def _():
-            dn_message(i, 0, 0, source).wait_recv()
-            zacc[...] = zacc[...] - nt(dn_recv[i], wall[i + 2 * joined])
+            da[...] = zp_recv[...]
+
+        for i in range(2):
+
+            @pl.when(jnp.logical_and(jnp.logical_not(is_plain), inside(group_host(i))))
+            def _():
+                v_message(0, 0, i, group_host(i)).wait_recv()
+
+                @pl.when(is_skipped)
+                def _():
+                    zacc[...] = zacc[...] - dv_recv[i].astype(F32)
+
+                @pl.when(is_joined)
+                def _():
+                    da[...] = (da[...].astype(F32) - dv_recv[i].astype(F32)).astype(BF)
+
+        @pl.when(is_joined)
+        def _():
+            @pl.when(level + 1 == lowest)
+            def _():
+                da_message(leaf + (2 * near - 1) * half_span).start()
+
+            zacc[...] = zacc[...] - nt(da[...], wall[near])
 
     draws = zacc[...]
     sep_out[...] = draws
@@ -597,32 +671,64 @@
 
     def for_level(h, act):
         below = lax.shift_left(jnp.int32(1), jnp.int32(h))
-        ahead = any_of(jnp.int32(h) + 1, skipped)
+        bypassed = jnp.logical_or(
+            any_of(jnp.int32(h), skipped), jnp.logical_and(is_skipped, h >= level - 2)
+        )
         for i in range(2):
             target = leaf + (1 - 2 * i) * below
-            target3 = leaf + (1 - 2 * i) * 3 * below
-            passed = jnp.logical_and(ahead, level == h + 1)
-
-            @pl.when(jnp.logical_and(jnp.logical_not(passed), inside(target)))
-            def _():
-                act(dn_message(i, 0, h, target))
-
-            if skipped:
-
-                @pl.when(
-                    jnp.logical_and(jnp.logical_and(ahead, level > h + 1), inside(target3))
-                )
-                def _():
-                    act(dn_message(i, 1, h, target3))
-
-    @pl.loop(0, level)
+
+            @pl.when(jnp.logical_and(jnp.logical_not(bypassed), inside(target)))
+            def _():
+                act(dn_message(i, h, target))
+
+    def begin(message):
+        message.start()
+
+    def left(message):
+        message.wait_send()
+
+    steps = jnp.maximum(level - lowest + 1, 0)
+
+    @pl.loop(0, steps)
     def _(step):
-        for_level(level - 1 - step, lambda message: message.start())
-        for_level(level - 1 - step, lambda message: message.wait_send())
+        for_level(level - 1 - step, begin)
+
+    if skipped:
+
+        def to_group(slot):
+            center, reach = group_of(slot)
+            return [
+                v_message(slot, which, group_side(slot), target)
+                for which, target in enumerate((center - reach, center + reach, center))
+            ]
+
+        for slot in range(2):
+
+            @pl.when(has_group(slot))
+            def _():
+                v_send[slot] = nt(dn_send[...], hw[slot]).astype(BF)
+                for message in to_group(slot):
+                    message.start()
+
+        for slot in range(2):
+
+            @pl.when(has_group(slot))
+            def _():
+                for message in to_group(slot):
+                    message.wait_send()
+
+    @pl.loop(0, steps)
+    def _(step):
+        for_level(level - 1 - step, left)
+
+    @pl.loop(steps, level)
+    def _(step):
+        for_level(level - 1 - step, begin)
+        for_level(level - 1 - step, left)
 
     @pl.when(is_even)
     def _():
-        dn_message(2, 0, 0, leaf + 1).start()
+        dn_message(2, 0, leaf + 1).start()
 
     own_dup[0:HALF] = dn_send[...]
     own_dup[HALF:] = dn_send[...]
@@ -639,7 +745,7 @@
 
     @pl.when(jnp.logical_not(is_even))
     def _():
-        dn_message(2, 0, 0, leaf - 1).wait_recv()
+        dn_message(2, 0, leaf - 1).wait_recv()
         prev_dup[0:HALF] = dn_recv[2]
 
     @pl.when(jnp.logical_and(is_even, leaf > 0))
@@ -689,25 +795,38 @@
 
         @pl.when(inside(target))
         def _():
-            up_message(i, i, far_of(i), own_level, target).wait_send()
+            up_message(i, own_level, target).wait_send()
 
     @pl.when(is_even)
     def _():
-        dn_message(2, 0, 0, leaf + 1).wait_send()
+        dn_message(2, 0, leaf + 1).wait_send()
 
     if skipped:
 
         @pl.when(is_joined)
         def _():
-            up_message(2, near, 0, own_level, parent).wait_send()
-            cx_copy(core).wait_send()
+            for side in range(2):
+
+                @pl.when(inside(group_host(side)))
+                def _():
+                    to_host(side).wait_send()
+
+            @pl.when(level + 1 == lowest)
+            def _():
+                da_message(leaf + (2 * near - 1) * half_span).wait_send()
 
         @pl.when(is_skipped)
         def _():
             for i in range(2):
-                child = leaf + (1 - 2 * i) * half_span
-                wa_copy(i, child).wait_send()
-                zp_message(i, child).wait_send()
+                zp_message(i, leaf + (1 - 2 * i) * half_span).wait_send()
+
+                @pl.when(inside(ancestor(i)))
+                def _():
+                    hw_copy(i, host_slot(i), ancestor(i)).wait_send()
+
+        @pl.when(is_host)
+        def _():
+            gather_host.drain()
 
 
 def on_device(
@@ -755,7 +874,7 @@
             pltpu.VMEM((share, width), BF),
             pltpu.VMEM((width, width), BF),
             pltpu.VMEM((2, width, width), BF),
-            pltpu.VMEM((4, width, width), BF),
+            pltpu.VMEM((2, width, width), BF),
             pltpu.VMEM((2, width, width), BF),
             pltpu.VMEM((2, order, 128), BF),
             pltpu.VMEM((share, width), F32),
@@ -763,11 +882,15 @@
             pltpu.VMEM((share, width), F32),
             pltpu.VMEM((share, width), BF),
             pltpu.VMEM((share, width), BF),
-            pltpu.VMEM((3, share, width), BF),
-            pltpu.VMEM((2, depth, 2, share, width), BF),
+            pltpu.VMEM((2, share, width), BF),
+            pltpu.VMEM((depth, 2, share, width), BF),
             pltpu.VMEM((share, width), BF),
             pltpu.VMEM((3, share, width), BF),
             pltpu.VMEM((share, width), BF),
+            pltpu.VMEM((share, width), BF),
+            pltpu.VMEM((2, 2, share, width), BF),
+            pltpu.VMEM((2, share, width), BF),
+            pltpu.VMEM((2, share, width), BF),
             pltpu.VMEM((share, width), BF),
             pltpu.VMEM((2 * share, width), BF),
             pltpu.VMEM((2 * share, width), BF),
@@ -785,16 +908,21 @@
             dma((2, 9)),
             dma,
             dma,
-            dma((3, 2)),
-            dma((2, depth, 2, 2)),
-            dma((2, 3, depth, 2)),
+            dma((2, 2)),
+            dma((depth, 2, 2)),
+            dma((3, depth, 2)),
             dma((3, 2)),
             dma((n_front - 1,)),
             dma((n_front - 1,)),
             dma((2,)),
-            dma,
-            dma,
-            dma,
+            dma((2,)),
+            dma((9,)),
+            dma((9,)),
+            dma((2, 2)),
+            dma((2, 2, 2)),
+            dma((2, 3, 2)),
+            dma((2, 2)),
+            dma((2,)),
             dma((2, 2)),
             dma((2,)),
             pltpu.SemaphoreType.REGULAR,

time: 124 us -> 110 us (0.89)
  the two profiles are of different devices: /device:TPU:1 before, /device:TPU:41 now
where the time goes in v3:
time: 110 us; the launch traced here: 109 us
  Pallas kernels  103 us (94%)
  local copies, waits for them, and re-layouts  4.2 us (4%)
  between operations  1.29 us (1%)
    pallas_call x1, Pallas kernels, on_device(): pl.pallas_call(functools.partial(kernel, n_leaf, n_front, depth), out_sha...  103 us
    unnamed x2, local copies, waits for them, and re-layouts  2.49 us

profile of v3, /device:TPU:41, one launch (start us, length us, event | category | flops | bytes accessed | tf_op | source)
XLA Modules:
  0.0 109.5 jit_solution(18081350774244534773)
XLA Ops:
  1.3 1.7 %copy_bitcast_fusion = (bf16[4,32,512]{2,1,0:T(8,128)(2,1)}, bf16[4,32,512]{2,1,0:T(8,128)(2,1)}) fusion(bf16[1,32,4,512]{3,2,1,0:T(4,128)(2,1)} %param.13, bf16[1,32,4,512]{3,2,1,0:T(4,128)(2,1)} %param.11), kind=kLoop, calls=%fused_computation.1 | loop fusion | bytes 524288 | tf_op jit(solution)/shard_map/transpose | solution.py:852
  3.0 103.1 %shard_map.122 = (bf16[4,32,512]{2,1,0:T(8,128)(2,1)}, f32[64,768]{1,0:T(8,128)}) custom-call(s32[1]{0:T(128)S(6)} %copy.19.cnt_ref, bf16[4,32,512]{2,1,0:T(8,128)(2,1)} %get-tuple-element.9.rhs_hbm, bf16[4,32,512]{2,1,0:T(8,128)(2,1)} %get-tuple-element.8.noise_hbm, bf16[4,32,256]{2,1,0:T(8,128)(2,1)} %bitcast.29, bf16[4,32,768]{2,1,0:T(8,128)(2,1)} %bitcast.24, ...), custom_call_target="tpu_custom_call" | custom-call | tf_op jit(solution)/shard_map/pallas_call | solution.py:856
  106.1 0.9 convert_bitcast_fusion
  107.0 0.9 copy.15
  107.9 1.6 %copy.20 = f32[1,64,768]{2,1,0:T(8,128)} copy(f32[1,64,768]{2,1,0:T(8,128)} %bitcast.26) | data formatting | bytes 393216

commit v4 on v3

--- a/solution.py
+++ b/solution.py
@@ -26,8 +26,10 @@
     return lax.dot_general(a, b, (((0,), (0,)), ((), ())), preferred_element_type=F32)
 
 
-def pack(block_ref, packed_ref):
-    _, rows, samples = block_ref.shape
+def pack(raw_ref, block_ref, packed_ref):
+    rows, slots, samples = raw_ref.shape
+    for t in range(slots):
+        block_ref[t] = raw_ref[:, t, :]
     for slab in range(samples // 128):
         lanes = slice(slab * 128, slab * 128 + 128)
         a = block_ref[0:2, :, lanes].reshape(2 * rows, 128)
@@ -57,6 +59,7 @@
     sep_out,
     x_buf,
     n_buf,
+    turned_slots,
     pk,
     pkn,
     r2,
@@ -68,7 +71,9 @@
     sinv,
     su,
     wall,
+    wt,
     hw,
+    hwt,
     s2,
     res,
     rb,
@@ -125,7 +130,7 @@
     chips = n_front // 2
     x = front // 2
     core = front % 2
-    rows = x_buf.shape[1]
+    rows = x_buf.shape[0]
     pos = leaf + 1
     level = jnp.int32(0)
     for bit in range(1, depth + 1):
@@ -151,6 +156,7 @@
     joined = is_joined.astype(jnp.int32)
     near = ((pos // span) % 4 == 1).astype(jnp.int32)
     parent = leaf + (2 * near - 1) * span
+    parent_near = (((parent + 1) // (2 * span)) % 4 == 1).astype(jnp.int32)
     own_level = jnp.minimum(level, depth - 1)
     half_span = jnp.maximum(span // 2, 1)
     lowest = skipped[0] if skipped else depth
@@ -232,7 +238,7 @@
             pl.semaphore_signal(barrier, inc=1, device_id={"leaf": target}, device_id_type=MESH)
 
     loads[0].wait()
-    pack(x_buf, pk)
+    pack(x_buf, turned_slots, pk)
     loads[4].wait()
     loads[5].wait()
     wall[0] = tn(sinv[...], su[0]).astype(BF)
@@ -490,15 +496,23 @@
                         message.parts[n].start()
                     else:
 
-                        @pl.when(is_joined)
+                        @pl.when(jnp.logical_not(is_joined))
                         def _():
-                            for side in range(2):
-
-                                @pl.when(inside(group_host(side)))
-                                def _():
-                                    to_host(side).parts[n].start()
-
-                        message.parts[n].start()
+                            message.parts[n].start()
+
+                        @pl.when(jnp.logical_and(is_joined, inside(group_host(parent_near))))
+                        def _():
+                            to_host(parent_near).parts[n].start()
+
+        if skipped:
+
+            @pl.when(is_joined)
+            def _():
+                @pl.when(inside(group_host(1 - parent_near)))
+                def _():
+                    to_host(1 - parent_near).start()
+
+                up_message(near, own_level, parent).start()
 
     def to_host(side):
         return hu_message(side, host_slot(side), 1 - near, group_host(side))
@@ -619,10 +633,22 @@
                 zp_message(i, leaf + (1 - 2 * i) * half_span).start()
 
     loads[9].wait()
-    pack(n_buf, pkn)
+    pack(n_buf, turned_slots, pkn)
     for step in range(1, n_front):
         exchange(pkn, rows_of(n2), nz_send, nz_recv, step).start()
     n2[:, own_rows, :] = pkn[front]
+    for i in range(2):
+        wt[i] = wall[i].T
+    if skipped:
+
+        @pl.when(is_host)
+        def _():
+            for slot in range(2):
+
+                @pl.when(has_group(slot))
+                def _():
+                    hwt[slot] = hw[slot].T
+
 
     is_plain = jnp.logical_not(jnp.logical_or(is_skipped, is_joined))
 
@@ -632,10 +658,9 @@
         @pl.when(jnp.logical_and(wanted, inside(source)))
         def _():
             dn_message(i, 0, source).wait_recv()
-            zacc[...] = zacc[...] - nt(dn_recv[i], wall[i])
+            zacc[...] = zacc[...] - nn(dn_recv[i], wt[i])
 
     take_draws(1 - near, jnp.logical_not(is_skipped))
-    take_draws(near, is_plain)
     if skipped:
 
         @pl.when(is_joined)
@@ -663,11 +688,43 @@
             def _():
                 da_message(leaf + (2 * near - 1) * half_span).start()
 
-            zacc[...] = zacc[...] - nt(da[...], wall[near])
-
-    draws = zacc[...]
-    sep_out[...] = draws
-    dn_send[...] = draws.astype(BF)
+            dn_recv[near] = da[...]
+
+    plain_last = jnp.logical_and(is_plain, inside(ancestor(near)))
+
+    @pl.when(plain_last)
+    def _():
+        dn_message(near, 0, ancestor(near)).wait_recv()
+
+    is_early = jnp.logical_and(level > 0, level < lowest)
+
+    def early(act):
+        for i in range(2):
+            target = leaf + (1 - 2 * i) * half_span
+
+            @pl.when(jnp.logical_and(is_early, inside(target)))
+            def _():
+                act(dn_message(i, jnp.maximum(level - 1, 0), target))
+
+        @pl.when(is_even)
+        def _():
+            act(dn_message(2, 0, leaf + 1))
+
+    has_last = jnp.logical_or(plain_last, is_joined)
+
+    @pl.when(has_last)
+    def _():
+        for n, (low, high) in enumerate(chunks):
+            value = zacc[:, low:high] - nn(dn_recv[near], wt[near, :, low:high])
+            zacc[:, low:high] = value
+            dn_send[:, low:high] = value.astype(BF)
+            early(lambda message: message.parts[n].start())
+
+    @pl.when(jnp.logical_not(has_last))
+    def _():
+        dn_send[...] = zacc[...].astype(BF)
+
+    sep_out[...] = zacc[...]
 
     def for_level(h, act):
         below = lax.shift_left(jnp.int32(1), jnp.int32(h))
@@ -702,11 +759,11 @@
                 for which, target in enumerate((center - reach, center + reach, center))
             ]
 
-        for slot in range(2):
+        for slot in (1, 0):
 
             @pl.when(has_group(slot))
             def _():
-                v_send[slot] = nt(dn_send[...], hw[slot]).astype(BF)
+                v_send[slot] = nn(dn_send[...], hwt[slot]).astype(BF)
                 for message in to_group(slot):
                     message.start()
 
@@ -721,14 +778,12 @@
     def _(step):
         for_level(level - 1 - step, left)
 
-    @pl.loop(steps, level)
+    early(left)
+
+    @pl.loop(steps + is_early.astype(jnp.int32), level)
     def _(step):
         for_level(level - 1 - step, begin)
         for_level(level - 1 - step, left)
-
-    @pl.when(is_even)
-    def _():
-        dn_message(2, 0, leaf + 1).start()
 
     own_dup[0:HALF] = dn_send[...]
     own_dup[HALF:] = dn_send[...]
@@ -773,10 +828,10 @@
     for t in range(2):
         for slab in range(n_front // 2):
             lanes = slice(slab * 128, slab * 128 + 128)
-            a = o2[2 * slab, t]
-            b = o2[2 * slab + 1, t]
-            leaf_out[t, :, lanes] = jnp.concatenate([a[:, :HALF], b[:, :HALF]], axis=1)
-            leaf_out[t + 2, :, lanes] = jnp.concatenate([a[:, HALF:], b[:, HALF:]], axis=1)
+            a = o2[2 * slab, t].astype(F32)
+            b = o2[2 * slab + 1, t].astype(F32)
+            leaf_out[:, t, lanes] = jnp.concatenate([a[:, :HALF], b[:, :HALF]], axis=1)
+            leaf_out[:, t + 2, lanes] = jnp.concatenate([a[:, HALF:], b[:, HALF:]], axis=1)
 
     for step in range(1, n_front):
         exchange(pk, rows_of(r2), a_send, a_recv, step).wait_send()
@@ -796,10 +851,6 @@
         @pl.when(inside(target))
         def _():
             up_message(i, own_level, target).wait_send()
-
-    @pl.when(is_even)
-    def _():
-        dn_message(2, 0, leaf + 1).wait_send()
 
     if skipped:
 
@@ -848,21 +899,20 @@
     _, rows, slots, samples = leaf_rhs.shape
     share, width = sep_rhs.shape[1:]
     order = rows * n_front
-    rhs = jnp.transpose(leaf_rhs[0], (1, 0, 2))
-    noise = jnp.transpose(leaf_noise[0], (1, 0, 2))
     hbm = pl.BlockSpec(memory_space=pltpu.HBM)
     vmem = pl.BlockSpec(memory_space=pltpu.VMEM)
     dma = pltpu.SemaphoreType.DMA
     leaf_draws, sep_draws = pl.pallas_call(
         functools.partial(kernel, n_leaf, n_front, depth),
         out_shape=(
-            jax.ShapeDtypeStruct((slots, rows, samples), BF),
+            jax.ShapeDtypeStruct((rows, slots, samples), F32),
             jax.ShapeDtypeStruct((share, width), F32),
         ),
         in_specs=[pl.BlockSpec(memory_space=pltpu.SMEM)] + [hbm] * 10,
         out_specs=(vmem, vmem),
         scratch_shapes=[
-            pltpu.VMEM((slots, rows, samples), BF),
+            pltpu.VMEM((rows, slots, samples), BF),
+            pltpu.VMEM((rows, slots, samples), BF),
             pltpu.VMEM((slots, rows, samples), BF),
             pltpu.VMEM((n_front, 2, rows, 128), BF),
             pltpu.VMEM((n_front, 2, rows, 128), BF),
@@ -873,6 +923,8 @@
             pltpu.VMEM((share, width), BF),
             pltpu.VMEM((share, width), BF),
             pltpu.VMEM((width, width), BF),
+            pltpu.VMEM((2, width, width), BF),
+            pltpu.VMEM((2, width, width), BF),
             pltpu.VMEM((2, width, width), BF),
             pltpu.VMEM((2, width, width), BF),
             pltpu.VMEM((2, width, width), BF),
@@ -932,8 +984,8 @@
         ),
     )(
         leaf_count,
-        rhs,
-        noise,
+        leaf_rhs[0],
+        leaf_noise[0],
         leaf_inverse[0],
         leaf_left[0],
         leaf_right[0],
@@ -943,7 +995,6 @@
         sep_left[0],
         sep_right[0],
     )
-    leaf_draws = jnp.transpose(leaf_draws, (1, 0, 2)).astype(F32)
     return (leaf_draws[None], sep_draws[None])
 
 

time: 110 us -> 109 us (level)
  the two profiles are of different devices: /device:TPU:41 before, /device:TPU:1 now
where the time goes in v4:
time: 109 us
  Pallas kernels  104 us (95%)
  local copies, waits for them, and re-layouts  3.29 us (3%)
  between operations  1.29 us (1%)
    pallas_call x1, Pallas kernels, on_device(): pl.pallas_call(functools.partial(kernel, n_leaf, n_front, depth), out_sha...  104 us
    unnamed x2, local copies, waits for them, and re-layouts  3.29 us

profile of v4, /device:TPU:1, one launch (start us, length us, event | category | flops | bytes accessed | tf_op | source)
XLA Modules:
  0.0 108.8 jit_solution(15636317186137413381)
XLA Ops:
  1.3 104.2 %shard_map.122 = (f32[32,4,512]{2,1,0:T(4,128)}, f32[64,768]{1,0:T(8,128)}) custom-call(s32[1]{0:T(128)S(6)} %copy.15.cnt_ref, bf16[32,4,512]{2,1,0:T(4,128)(2,1)} %bitcast.19, bf16[32,4,512]{2,1,0:T(4,128)(2,1)} %bitcast.20, bf16[4,32,256]{2,1,0:T(8,128)(2,1)} %bitcast.23, bf16[4,32,768]{2,1,0:T(8,128)(2,1)} %bitcast.16, bf16[4,32,768]{2,1,0:T(8,128)(2,1)} %bitcast.17, ...), custom_call_target="tpu_custom_call" | custom-call | tf_op jit(solution)/shard_map/pallas_call | solution.py:905
  105.5 1.7 %copy.16 = f32[1,32,4,512]{3,2,1,0:T(4,128)} copy(f32[1,32,4,512]{3,2,1,0:T(4,128)} %bitcast.15) | data formatting | bytes 524288
  107.2 1.6 %copy.17 = f32[1,64,768]{2,1,0:T(8,128)} copy(f32[1,64,768]{2,1,0:T(8,128)} %bitcast.18) | data formatting | bytes 393216

commit v5 on v4

--- a/solution.py
+++ b/solution.py
@@ -140,6 +140,7 @@
         span = jnp.where(pos % (1 << bit) == 0, jnp.int32(1 << bit), span)
     odd = leaf % 2
     is_even = odd == 0
+    is_root = level == depth
 
     def inside(target):
         return jnp.logical_and(target >= 0, target < n_leaf)
@@ -375,6 +376,7 @@
     gather_inv.send(4, 3)
     gather_inv.take(1)
     gather_inv.send(6, 5)
+    gather_two.send(0, 1, 2)
     if skipped:
 
         @pl.when(is_skipped)
@@ -394,7 +396,6 @@
     gather_inv.send(7)
     gather_inv.take(6)
     gather_inv.send(8)
-    gather_two.send(0, 1, 2)
     for step in range(1, n_front):
         arrival(pk, rows_of(r2), a_send, a_recv, step).wait_recv()
     gather_inv.take(2, 3, 5, 7, 8)
@@ -593,6 +594,12 @@
                 gather_host.take(6)
                 gather_host.send(8)
 
+        @pl.when(is_root)
+        def _():
+            loads[8].wait()
+            su[0] = tn(sinv[...], sinv[...]).astype(BF)
+            zacc[...] = nn(snoise[...], sinv[...])
+
         @pl.loop(0, level - is_skipped.astype(jnp.int32))
         def _(h):
             gather_level(h)
@@ -620,10 +627,17 @@
                 gather_level(level - 1)
                 rb[...] = res[...].astype(BF)
 
-    loads[8].wait()
-    solved_sep = nt(rb[...], sinv[...]).astype(BF).astype(F32)
-    target_sep = (solved_sep + snoise[...].astype(F32)).astype(BF)
-    zacc[...] = nn(target_sep, sinv[...])
+    @pl.when(is_root)
+    def _():
+        zacc[...] = zacc[...] + nn(rb[...], su[0])
+
+    @pl.when(jnp.logical_not(is_root))
+    def _():
+        loads[8].wait()
+        solved_sep = nt(rb[...], sinv[...]).astype(BF).astype(F32)
+        target_sep = (solved_sep + snoise[...].astype(F32)).astype(BF)
+        zacc[...] = nn(target_sep, sinv[...])
+
     if skipped:
 
         @pl.when(is_skipped)
@@ -878,6 +892,17 @@
         @pl.when(is_host)
         def _():
             gather_host.drain()
+
+
+def hand_over(leaf_in, sep_in, leaf_ref, sep_ref, sems):
+    copies = [
+        pltpu.make_async_copy(leaf_in, leaf_ref, sems.at[0]),
+        pltpu.make_async_copy(sep_in, sep_ref, sems.at[1]),
+    ]
+    for copy in copies:
+        copy.start()
+    for copy in copies:
+        copy.wait()
 
 
 def on_device(
@@ -995,6 +1020,17 @@
         sep_left[0],
         sep_right[0],
     )
+    leaf_draws, sep_draws = pl.pallas_call(
+        hand_over,
+        out_shape=(
+            jax.ShapeDtypeStruct(leaf_draws.shape, F32),
+            jax.ShapeDtypeStruct(sep_draws.shape, F32),
+        ),
+        in_specs=[hbm, hbm],
+        out_specs=(hbm, hbm),
+        scratch_shapes=[dma((2,))],
+        compiler_params=pltpu.CompilerParams(vmem_limit_bytes=63 * 1024 * 1024),
+    )(leaf_draws, sep_draws)
     return (leaf_draws[None], sep_draws[None])
 
 

time: 109 us -> 121 us (1.11)
  Pallas kernels: 104 us -> 120 us
  local copies, waits for them, and re-layouts: 3.29 us -> 0 us
    pallas_call x0 -> x1, Pallas kernels: none -> 15 us  [on_device(): pl.pallas_call(hand_over, out_shape=(jax.ShapeDtypeStruct(leaf_draws.shap...]
    unnamed x2 -> x0, local copies, waits for them, and re-layouts: 3.29 us -> none
where the time goes in v5:
time: 121 us
  Pallas kernels  120 us (99%)
  between operations  1.29 us (1%)
    pallas_call x1, Pallas kernels, on_device(): pl.pallas_call(functools.partial(kernel, n_leaf, n_front, depth), out_sha...  105 us
    pallas_call x1, Pallas kernels, on_device(): pl.pallas_call(hand_over, out_shape=(jax.ShapeDtypeStruct(leaf_draws.shap...  15 us

profile of v5, /device:TPU:1, one launch (start us, length us, event | category | flops | bytes accessed | tf_op | source)
XLA Modules:
  0.0 121.4 jit_solution(2389615472055181080)
XLA Ops:
  1.3 105.0 %shard_map.122 = (f32[32,4,512]{2,1,0:T(4,128)}, f32[64,768]{1,0:T(8,128)}) custom-call(s32[1]{0:T(128)S(6)} %copy.13.cnt_ref, bf16[32,4,512]{2,1,0:T(4,128)(2,1)} %bitcast.17, bf16[32,4,512]{2,1,0:T(4,128)(2,1)} %bitcast.18, bf16[4,32,256]{2,1,0:T(8,128)(2,1)} %bitcast.21, bf16[4,32,768]{2,1,0:T(8,128)(2,1)} %bitcast.15, bf16[4,32,768]{2,1,0:T(8,128)(2,1)} %bitcast.16, ...), custom_call_target="tpu_custom_call" | custom-call | tf_op jit(solution)/shard_map/pallas_call | solution.py:930
  106.3 15.0 %shard_map.123 = (f32[32,4,512]{2,1,0:T(4,128)}, f32[64,768]{1,0:T(8,128)}) custom-call(f32[32,4,512]{2,1,0:T(4,128)} %get-tuple-element.6.leaf_in, f32[64,768]{1,0:T(8,128)} %get-tuple-element.7.sep_in), custom_call_target="tpu_custom_call" | custom-call | tf_op jit(solution)/shard_map/pallas_call | solution.py:1023

commit v6 on v4

--- a/solution.py
+++ b/solution.py
@@ -56,7 +56,8 @@
     sleft_hbm,
     sright_hbm,
     leaf_out,
-    sep_out,
+    sep_high,
+    sep_low,
     x_buf,
     n_buf,
     turned_slots,
@@ -140,6 +141,7 @@
         span = jnp.where(pos % (1 << bit) == 0, jnp.int32(1 << bit), span)
     odd = leaf % 2
     is_even = odd == 0
+    is_root = level == depth
 
     def inside(target):
         return jnp.logical_and(target >= 0, target < n_leaf)
@@ -593,6 +595,12 @@
                 gather_host.take(6)
                 gather_host.send(8)
 
+        @pl.when(is_root)
+        def _():
+            loads[8].wait()
+            su[0] = tn(sinv[...], sinv[...]).astype(BF)
+            zacc[...] = nn(snoise[...], sinv[...])
+
         @pl.loop(0, level - is_skipped.astype(jnp.int32))
         def _(h):
             gather_level(h)
@@ -620,10 +628,17 @@
                 gather_level(level - 1)
                 rb[...] = res[...].astype(BF)
 
-    loads[8].wait()
-    solved_sep = nt(rb[...], sinv[...]).astype(BF).astype(F32)
-    target_sep = (solved_sep + snoise[...].astype(F32)).astype(BF)
-    zacc[...] = nn(target_sep, sinv[...])
+    @pl.when(is_root)
+    def _():
+        zacc[...] = zacc[...] + nn(rb[...], su[0])
+
+    @pl.when(jnp.logical_not(is_root))
+    def _():
+        loads[8].wait()
+        solved_sep = nt(rb[...], sinv[...]).astype(BF).astype(F32)
+        target_sep = (solved_sep + snoise[...].astype(F32)).astype(BF)
+        zacc[...] = nn(target_sep, sinv[...])
+
     if skipped:
 
         @pl.when(is_skipped)
@@ -724,7 +739,8 @@
     def _():
         dn_send[...] = zacc[...].astype(BF)
 
-    sep_out[...] = zacc[...]
+    sep_high[...] = dn_send[...]
+    sep_low[...] = (zacc[...] - dn_send[...].astype(F32)).astype(BF)
 
     def for_level(h, act):
         below = lax.shift_left(jnp.int32(1), jnp.int32(h))
@@ -828,10 +844,11 @@
     for t in range(2):
         for slab in range(n_front // 2):
             lanes = slice(slab * 128, slab * 128 + 128)
-            a = o2[2 * slab, t].astype(F32)
-            b = o2[2 * slab + 1, t].astype(F32)
-            leaf_out[:, t, lanes] = jnp.concatenate([a[:, :HALF], b[:, :HALF]], axis=1)
-            leaf_out[:, t + 2, lanes] = jnp.concatenate([a[:, HALF:], b[:, HALF:]], axis=1)
+            a = o2[2 * slab, t]
+            b = o2[2 * slab + 1, t]
+            turned_slots[t, :, lanes] = jnp.concatenate([a[:, :HALF], b[:, :HALF]], axis=1)
+            turned_slots[t + 2, :, lanes] = jnp.concatenate([a[:, HALF:], b[:, HALF:]], axis=1)
+    leaf_out[...] = jnp.swapaxes(turned_slots[...], 0, 1)
 
     for step in range(1, n_front):
         exchange(pk, rows_of(r2), a_send, a_recv, step).wait_send()
@@ -902,14 +919,15 @@
     hbm = pl.BlockSpec(memory_space=pltpu.HBM)
     vmem = pl.BlockSpec(memory_space=pltpu.VMEM)
     dma = pltpu.SemaphoreType.DMA
-    leaf_draws, sep_draws = pl.pallas_call(
+    leaf_draws, sep_high, sep_low = pl.pallas_call(
         functools.partial(kernel, n_leaf, n_front, depth),
         out_shape=(
-            jax.ShapeDtypeStruct((rows, slots, samples), F32),
-            jax.ShapeDtypeStruct((share, width), F32),
+            jax.ShapeDtypeStruct((rows, slots, samples), BF),
+            jax.ShapeDtypeStruct((share, width), BF),
+            jax.ShapeDtypeStruct((share, width), BF),
         ),
         in_specs=[pl.BlockSpec(memory_space=pltpu.SMEM)] + [hbm] * 10,
-        out_specs=(vmem, vmem),
+        out_specs=(vmem, vmem, vmem),
         scratch_shapes=[
             pltpu.VMEM((rows, slots, samples), BF),
             pltpu.VMEM((rows, slots, samples), BF),
@@ -995,7 +1013,8 @@
         sep_left[0],
         sep_right[0],
     )
-    return (leaf_draws[None], sep_draws[None])
+    sep_draws = sep_high.astype(F32) + sep_low.astype(F32)
+    return (leaf_draws.astype(F32)[None], sep_draws[None])
 
 
 def solution(mesh):

time: 109 us -> 108 us (level)
  local copies, waits for them, and re-layouts: 3.29 us -> 0 us
  other arithmetic: 0 us -> 3.26 us
    unnamed x2 -> x0, local copies, waits for them, and re-layouts: 3.29 us -> none
    broadcast_in_dim x0 -> x2, other arithmetic: none -> 3.26 us  [on_device(): return (leaf_draws.astype(F32)[None], sep_draws[None])]
where the time goes in v6:
time: 108 us
  Pallas kernels  104 us (96%)
  other arithmetic  3.26 us (3%)
  between operations  1.29 us (1%)
    pallas_call x1, Pallas kernels, on_device(): pl.pallas_call(functools.partial(kernel, n_leaf, n_front, depth), out_sha...  104 us
    broadcast_in_dim x2, other arithmetic, on_device(): return (leaf_draws.astype(F32)[None], sep_draws[None])  3.26 us

profile of v6, /device:TPU:1, one launch (start us, length us, event | category | flops | bytes accessed | tf_op | source)
XLA Modules:
  0.0 108.2 jit_solution(6657192563847271786)
XLA Ops:
  1.3 103.7 %shard_map.122 = (bf16[32,4,512]{2,1,0:T(4,128)(2,1)}, bf16[64,768]{1,0:T(8,128)(2,1)}, bf16[64,768]{1,0:T(8,128)(2,1)}) custom-call(s32[1]{0:T(128)S(6)} %copy.13.cnt_ref, bf16[32,4,512]{2,1,0:T(4,128)(2,1)} %bitcast.20, bf16[32,4,512]{2,1,0:T(4,128)(2,1)} %bitcast.21, bf16[4,32,256]{2,1,0:T(8,128)(2,1)} %bitcast.24, bf16[4,32,768]{2,1,0:T(8,128)(2,1)} %bitcast.18, ...), custom_call_target="tpu_custom_call" | custom-call | tf_op jit(solution)/shard_map/pallas_call | solution.py:922
  105.0 1.6 %add_bitcast_fusion = f32[1,64,768]{2,1,0:T(8,128)} fusion(bf16[64,768]{1,0:T(8,128)(2,1)} %get-tuple-element.7, bf16[64,768]{1,0:T(8,128)(2,1)} %get-tuple-element.6), kind=kLoop, calls=%fused_computation | loop fusion | flops 147456 | bytes 393216 | tf_op jit(solution)/shard_map/broadcast_in_dim | solution.py:1017
  106.6 1.6 %bitcast_convert_fusion = f32[1,32,4,512]{3,2,1,0:T(4,128)} fusion(bf16[32,4,512]{2,1,0:T(4,128)(2,1)} %get-tuple-element.5), kind=kLoop, calls=%fused_computation.1 | loop fusion | flops 65536 | bytes 393216 | tf_op jit(solution)/shard_map/broadcast_in_dim | solution.py:1017

commit v7 on v6

--- a/solution.py
+++ b/solution.py
@@ -300,8 +300,8 @@
         return buf.at[low:high, pl.ds(pl.multiple_of(who * some, some), some), :]
 
     routes = [
-        (0, 0, 4, 1, False),
-        (0, 0, 4, -1, False),
+        (0, 0, 2, 1, False),
+        (0, 2, 4, -1, False),
         (0, 0, 4, 0, True),
         (-1, 0, 4, 0, True),
         (-1, 0, 2, 1, False),
@@ -309,6 +309,8 @@
         (1, 2, 4, -1, False),
         (2, 0, 2, 0, True),
         (2, 2, 4, 0, True),
+        (0, 2, 4, 1, False),
+        (0, 0, 2, -1, False),
     ]
 
     def route(buf, sends, recvs, i):
@@ -365,18 +367,22 @@
     for step in range(1, n_front):
         exchange(pk, rows_of(r2), a_send, a_recv, step).start()
     loads[1].wait()
-    gather_inv.send(0, 1, 2)
+    gather_inv.send(0, 1, 9, 10, 2)
     loads[2].wait()
     loads[3].wait()
-    gather_one.send(0, 1, 2)
+    gather_one.send(0, 1, 9, 10, 2)
     r2[:, own_rows, :] = pk[front]
 
     loads[6].wait()
     wall[1] = tn(sinv[...], su[1]).astype(BF)
     gather_inv.take(0)
-    gather_inv.send(4, 3)
+    gather_inv.send(4)
     gather_inv.take(1)
-    gather_inv.send(6, 5)
+    gather_inv.send(6)
+    gather_inv.take(9)
+    gather_inv.send(3)
+    gather_inv.take(10)
+    gather_inv.send(5)
     if skipped:
 
         @pl.when(is_skipped)
@@ -389,14 +395,18 @@
                     hw_copy(i, host_slot(i), ancestor(i)).start()
 
     gather_one.take(0)
-    gather_one.send(4, 3)
+    gather_one.send(4)
     gather_one.take(1)
-    gather_one.send(6, 5)
+    gather_one.send(6)
     gather_inv.take(4)
     gather_inv.send(7)
     gather_inv.take(6)
     gather_inv.send(8)
-    gather_two.send(0, 1, 2)
+    gather_one.take(9)
+    gather_one.send(3)
+    gather_one.take(10)
+    gather_one.send(5)
+    gather_two.send(0, 1, 9, 10, 2)
     for step in range(1, n_front):
         arrival(pk, rows_of(r2), a_send, a_recv, step).wait_recv()
     gather_inv.take(2, 3, 5, 7, 8)
@@ -543,9 +553,9 @@
         tl_copy(leaf - 1).start()
 
     gather_two.take(0)
-    gather_two.send(4, 3)
+    gather_two.send(4)
     gather_two.take(1)
-    gather_two.send(6, 5)
+    gather_two.send(6)
 
     @pl.when(is_even)
     def _():
@@ -554,6 +564,10 @@
         res[...] = res[...] - tl_recv[...].astype(F32)
         climb()
 
+    gather_two.take(9)
+    gather_two.send(3)
+    gather_two.take(10)
+    gather_two.send(5)
     gather_two.take(4)
     gather_two.send(7)
     gather_two.take(6)
@@ -585,11 +599,15 @@
                     def _():
                         hw_copy(0, slot, group_of(slot)[0]).wait_recv()
 
-                gather_host.send(0, 1, 2)
+                gather_host.send(0, 1, 9, 10, 2)
                 gather_host.take(0)
-                gather_host.send(4, 3)
+                gather_host.send(4)
                 gather_host.take(1)
-                gather_host.send(6, 5)
+                gather_host.send(6)
+                gather_host.take(9)
+                gather_host.send(3)
+                gather_host.take(10)
+                gather_host.send(5)
                 gather_host.take(4)
                 gather_host.send(7)
                 gather_host.take(6)
@@ -972,10 +990,10 @@
             dma((n_front - 1,)),
             dma((n_front - 1,)),
             dma((n_front - 1,)),
-            dma((9,)),
-            dma((9,)),
-            dma((2, 9)),
-            dma((2, 9)),
+            dma((11,)),
+            dma((11,)),
+            dma((2, 11)),
+            dma((2, 11)),
             dma,
             dma,
             dma((2, 2)),
@@ -986,8 +1004,8 @@
             dma((n_front - 1,)),
             dma((2,)),
             dma((2,)),
-            dma((9,)),
-            dma((9,)),
+            dma((11,)),
+            dma((11,)),
             dma((2, 2)),
             dma((2, 2, 2)),
             dma((2, 3, 2)),

time: 108 us -> 108 us (level)
  no operation moved by 1% of the time
where the time goes in v7:
time: 108 us; the launch traced here: 107 us
  Pallas kernels  103 us (95%)
  other arithmetic  3.26 us (3%)
  between operations  1.29 us (1%)
    pallas_call x1, Pallas kernels, on_device(): pl.pallas_call(functools.partial(kernel, n_leaf, n_front, depth), out_sha...  103 us
    broadcast_in_dim x2, other arithmetic, on_device(): return (leaf_draws.astype(F32)[None], sep_draws[None])  3.26 us

profile of v7, /device:TPU:1, one launch (start us, length us, event | category | flops | bytes accessed | tf_op | source)
XLA Modules:
  0.0 107.3 jit_solution(13673192729457671299)
XLA Ops:
  1.3 102.7 %shard_map.122 = (bf16[32,4,512]{2,1,0:T(4,128)(2,1)}, bf16[64,768]{1,0:T(8,128)(2,1)}, bf16[64,768]{1,0:T(8,128)(2,1)}) custom-call(s32[1]{0:T(128)S(6)} %copy.13.cnt_ref, bf16[32,4,512]{2,1,0:T(4,128)(2,1)} %bitcast.20, bf16[32,4,512]{2,1,0:T(4,128)(2,1)} %bitcast.21, bf16[4,32,256]{2,1,0:T(8,128)(2,1)} %bitcast.24, bf16[4,32,768]{2,1,0:T(8,128)(2,1)} %bitcast.18, ...), custom_call_target="tpu_custom_call" | custom-call | tf_op jit(solution)/shard_map/pallas_call | solution.py:940
  104.0 1.6 %add_bitcast_fusion = f32[1,64,768]{2,1,0:T(8,128)} fusion(bf16[64,768]{1,0:T(8,128)(2,1)} %get-tuple-element.7, bf16[64,768]{1,0:T(8,128)(2,1)} %get-tuple-element.6), kind=kLoop, calls=%fused_computation | loop fusion | flops 147456 | bytes 393216 | tf_op jit(solution)/shard_map/broadcast_in_dim | solution.py:1035
  105.6 1.6 %bitcast_convert_fusion = f32[1,32,4,512]{3,2,1,0:T(4,128)} fusion(bf16[32,4,512]{2,1,0:T(4,128)(2,1)} %get-tuple-element.5), kind=kLoop, calls=%fused_computation.1 | loop fusion | flops 65536 | bytes 393216 | tf_op jit(solution)/shard_map/broadcast_in_dim | solution.py:1035

commit v8 on v7

--- a/solution.py
+++ b/solution.py
@@ -552,6 +552,18 @@
         tl_send[...] = part_one.astype(BF)
         tl_copy(leaf - 1).start()
 
+    if skipped:
+
+        @pl.when(is_host)
+        def _():
+            for slot in range(2):
+
+                @pl.when(has_group(slot))
+                def _():
+                    hw_copy(0, slot, group_of(slot)[0]).wait_recv()
+
+            gather_host.send(0, 1, 9, 10, 2)
+
     gather_two.take(0)
     gather_two.send(4)
     gather_two.take(1)
@@ -568,6 +580,19 @@
     gather_two.send(3)
     gather_two.take(10)
     gather_two.send(5)
+    if skipped:
+
+        @pl.when(is_host)
+        def _():
+            gather_host.take(0)
+            gather_host.send(4)
+            gather_host.take(1)
+            gather_host.send(6)
+            gather_host.take(9)
+            gather_host.send(3)
+            gather_host.take(10)
+            gather_host.send(5)
+
     gather_two.take(4)
     gather_two.send(7)
     gather_two.take(6)
@@ -589,35 +614,20 @@
             tl_copy(leaf + 1).wait_recv()
             res[...] = res[...] - tl_recv[...].astype(F32)
 
+        @pl.when(is_root)
+        def _():
+            loads[8].wait()
+            su[0] = tn(sinv[...], sinv[...]).astype(BF)
+            zacc[...] = nn(snoise[...], sinv[...])
+
         if skipped:
 
             @pl.when(is_host)
             def _():
-                for slot in range(2):
-
-                    @pl.when(has_group(slot))
-                    def _():
-                        hw_copy(0, slot, group_of(slot)[0]).wait_recv()
-
-                gather_host.send(0, 1, 9, 10, 2)
-                gather_host.take(0)
-                gather_host.send(4)
-                gather_host.take(1)
-                gather_host.send(6)
-                gather_host.take(9)
-                gather_host.send(3)
-                gather_host.take(10)
-                gather_host.send(5)
                 gather_host.take(4)
                 gather_host.send(7)
                 gather_host.take(6)
                 gather_host.send(8)
-
-        @pl.when(is_root)
-        def _():
-            loads[8].wait()
-            su[0] = tn(sinv[...], sinv[...]).astype(BF)
-            zacc[...] = nn(snoise[...], sinv[...])
 
         @pl.loop(0, level - is_skipped.astype(jnp.int32))
         def _(h):

time: 108 us -> 108 us (level)
  no operation moved by 1% of the time
where the time goes in v8:
time: 108 us; the launch traced here: 107 us
  Pallas kernels  103 us (95%)
  other arithmetic  3.26 us (3%)
  between operations  1.29 us (1%)
    pallas_call x1, Pallas kernels, on_device(): pl.pallas_call(functools.partial(kernel, n_leaf, n_front, depth), out_sha...  103 us
    broadcast_in_dim x2, other arithmetic, on_device(): return (leaf_draws.astype(F32)[None], sep_draws[None])  3.26 us

profile of v8, /device:TPU:1, one launch (start us, length us, event | category | flops | bytes accessed | tf_op | source)
XLA Modules:
  0.0 107.3 jit_solution(3537197809863671545)
XLA Ops:
  1.3 102.7 %shard_map.122 = (bf16[32,4,512]{2,1,0:T(4,128)(2,1)}, bf16[64,768]{1,0:T(8,128)(2,1)}, bf16[64,768]{1,0:T(8,128)(2,1)}) custom-call(s32[1]{0:T(128)S(6)} %copy.13.cnt_ref, bf16[32,4,512]{2,1,0:T(4,128)(2,1)} %bitcast.20, bf16[32,4,512]{2,1,0:T(4,128)(2,1)} %bitcast.21, bf16[4,32,256]{2,1,0:T(8,128)(2,1)} %bitcast.24, bf16[4,32,768]{2,1,0:T(8,128)(2,1)} %bitcast.18, ...), custom_call_target="tpu_custom_call" | custom-call | tf_op jit(solution)/shard_map/pallas_call | solution.py:950
  104.0 1.6 %add_bitcast_fusion = f32[1,64,768]{2,1,0:T(8,128)} fusion(bf16[64,768]{1,0:T(8,128)(2,1)} %get-tuple-element.7, bf16[64,768]{1,0:T(8,128)(2,1)} %get-tuple-element.6), kind=kLoop, calls=%fused_computation | loop fusion | flops 147456 | bytes 393216 | tf_op jit(solution)/shard_map/broadcast_in_dim | solution.py:1045
  105.6 1.6 %bitcast_convert_fusion = f32[1,32,4,512]{3,2,1,0:T(4,128)} fusion(bf16[32,4,512]{2,1,0:T(4,128)(2,1)} %get-tuple-element.5), kind=kLoop, calls=%fused_computation.1 | loop fusion | flops 65536 | bytes 393216 | tf_op jit(solution)/shard_map/broadcast_in_dim | solution.py:1045

commit v9 on v8

--- a/solution.py
+++ b/solution.py
@@ -266,6 +266,8 @@
         def _():
             pl.semaphore_signal(known_sem, inc=1, device_id={"leaf": parent}, device_id_type=MESH)
 
+    far_first = sorted(range(1, n_front), key=lambda step: abs(step - n_front // 2))
+
     def exchange(src, dst_at, sends, recvs, step):
         peer = (front + step) % n_front
         return pltpu.make_async_remote_copy(
@@ -364,7 +366,7 @@
     gather_one = Gather(lw.at[first], g_send.at[0], g_recv.at[0])
     gather_two = Gather(lw.at[second], g_send.at[1], g_recv.at[1])
 
-    for step in range(1, n_front):
+    for step in far_first:
         exchange(pk, rows_of(r2), a_send, a_recv, step).start()
     loads[1].wait()
     gather_inv.send(0, 1, 9, 10, 2)
@@ -861,19 +863,20 @@
         mixed = jnp.where(alive[t], mixed, 0.0).astype(BF)
         drawn = jnp.where(low_lanes, tn(inv[t], mixed), tn(inv[t + 2], mixed)).astype(BF)
         for f in range(n_front):
-            d2[f, t] = drawn[f * rows : f * rows + rows]
-
-    for step in range(1, n_front):
-        exchange(d2, lambda f: o2.at[f], o_send, o_recv, step).start()
-    o2[front] = d2[front]
-    for step in range(1, n_front):
-        arrival(d2, lambda f: o2.at[f], o_send, o_recv, step).wait_recv()
+            d2[t, f] = drawn[f * rows : f * rows + rows]
+        for step in far_first:
+            exchange(d2.at[t], lambda f: o2.at[t, f], o_send.at[t], o_recv.at[t], step).start()
+        o2[t, front] = d2[t, front]
+
+    for t in range(2):
+        for step in range(1, n_front):
+            arrival(d2.at[t], lambda f: o2.at[t, f], o_send.at[t], o_recv.at[t], step).wait_recv()
 
     for t in range(2):
         for slab in range(n_front // 2):
             lanes = slice(slab * 128, slab * 128 + 128)
-            a = o2[2 * slab, t]
-            b = o2[2 * slab + 1, t]
+            a = o2[t, 2 * slab]
+            b = o2[t, 2 * slab + 1]
             turned_slots[t, :, lanes] = jnp.concatenate([a[:, :HALF], b[:, :HALF]], axis=1)
             turned_slots[t + 2, :, lanes] = jnp.concatenate([a[:, HALF:], b[:, HALF:]], axis=1)
     leaf_out[...] = jnp.swapaxes(turned_slots[...], 0, 1)
@@ -881,7 +884,8 @@
     for step in range(1, n_front):
         exchange(pk, rows_of(r2), a_send, a_recv, step).wait_send()
         exchange(pkn, rows_of(n2), nz_send, nz_recv, step).wait_send()
-        exchange(d2, lambda f: o2.at[f], o_send, o_recv, step).wait_send()
+        for t in range(2):
+            exchange(d2.at[t], lambda f: o2.at[t, f], o_send.at[t], o_recv.at[t], step).wait_send()
     gather_inv.drain()
     gather_one.drain()
     gather_two.drain()
@@ -993,8 +997,8 @@
             pltpu.VMEM((2 * share, width), BF),
             pltpu.VMEM((2 * share, width), BF),
             pltpu.VMEM((2, order, 128), F32),
-            pltpu.VMEM((n_front, 2, rows, 128), BF),
-            pltpu.VMEM((n_front, 2, rows, 128), BF),
+            pltpu.VMEM((2, n_front, rows, 128), BF),
+            pltpu.VMEM((2, n_front, rows, 128), BF),
             dma((10,)),
             dma((n_front - 1,)),
             dma((n_front - 1,)),
@@ -1010,8 +1014,8 @@
             dma((depth, 2, 2)),
             dma((3, depth, 2)),
             dma((3, 2)),
-            dma((n_front - 1,)),
-            dma((n_front - 1,)),
+            dma((2, n_front - 1)),
+            dma((2, n_front - 1)),
             dma((2,)),
             dma((2,)),
             dma((11,)),

time: 108 us -> 108 us (level)
  no operation moved by 1% of the time
where the time goes in v9:
time: 108 us; the launch traced here: 107 us
  Pallas kernels  103 us (95%)
  other arithmetic  3.26 us (3%)
  between operations  1.29 us (1%)
    pallas_call x1, Pallas kernels, on_device(): pl.pallas_call(functools.partial(kernel, n_leaf, n_front, depth), out_sha...  103 us
    broadcast_in_dim x2, other arithmetic, on_device(): return (leaf_draws.astype(F32)[None], sep_draws[None])  3.26 us

profile of v9, /device:TPU:1, one launch (start us, length us, event | category | flops | bytes accessed | tf_op | source)
XLA Modules:
  0.0 107.2 jit_solution(12869746462041038544)
XLA Ops:
  1.3 102.6 %shard_map.122 = (bf16[32,4,512]{2,1,0:T(4,128)(2,1)}, bf16[64,768]{1,0:T(8,128)(2,1)}, bf16[64,768]{1,0:T(8,128)(2,1)}) custom-call(s32[1]{0:T(128)S(6)} %copy.13.cnt_ref, bf16[32,4,512]{2,1,0:T(4,128)(2,1)} %bitcast.20, bf16[32,4,512]{2,1,0:T(4,128)(2,1)} %bitcast.21, bf16[4,32,256]{2,1,0:T(8,128)(2,1)} %bitcast.24, bf16[4,32,768]{2,1,0:T(8,128)(2,1)} %bitcast.18, ...), custom_call_target="tpu_custom_call" | custom-call | tf_op jit(solution)/shard_map/pallas_call | solution.py:954
  103.9 1.6 %add_bitcast_fusion = f32[1,64,768]{2,1,0:T(8,128)} fusion(bf16[64,768]{1,0:T(8,128)(2,1)} %get-tuple-element.7, bf16[64,768]{1,0:T(8,128)(2,1)} %get-tuple-element.6), kind=kLoop, calls=%fused_computation | loop fusion | flops 147456 | bytes 393216 | tf_op jit(solution)/shard_map/broadcast_in_dim | solution.py:1049
  105.5 1.6 %bitcast_convert_fusion = f32[1,32,4,512]{3,2,1,0:T(4,128)} fusion(bf16[32,4,512]{2,1,0:T(4,128)(2,1)} %get-tuple-element.5), kind=kLoop, calls=%fused_computation.1 | loop fusion | flops 65536 | bytes 393216 | tf_op jit(solution)/shard_map/broadcast_in_dim | solution.py:1049
